TPU v7x, 32 devices: a whole 2x2x4 slice. The times are simulated.
32 devices in a mesh: chan: 8 (over z, x), hour: 4 (over y, core).
Axes of the slice: x: 2, y: 2, z: 4, core: 2. Of those that a mesh axis runs over, the one named last changes fastest.
Arguments:
- traces: bfloat16 [1024, 16384], P('chan', 'hour'), may hold values from -6 to 6
- taps: bfloat16 [1024, 512], P('chan'), may hold values from -0.25 to 0.25
- bin_ids: int32 [4, 8], P(None, 'chan'), may hold values from 0 to 31
- owners: int32 [32], replicated, may hold values from 0 to 31, each once
Outputs:
- stacks: float32 [32, 8192], P(('chan', 'hour'))
Inputs may be any that keep to these rules, and one draw needn't show every extreme that they name: bin_ids[r, i] is the distance bin of the pair of block i - r - 1 with block i; entries with i <= r name no pair and are not read. owners is a permutation: bin b is held in row owners[b] of stacks.
All inputs are finite; a program needn't handle non-finite values.
Results may differ from a plain program's by a relative error of at most 0.004.
Values may be sent and summed in bfloat16 or wider, within the bound.
A program may use at most 256 MiB of HBM per device.

v0:
```python
import math

import jax
import jax.numpy as jnp
from jax import lax
from jax.sharding import PartitionSpec as P

FR = 4096
ROUNDS = 4


exact = lax.Precision.HIGHEST


def passed_along(shard, axis, by):
    devices = lax.axis_size(axis)
    pairs = [(i, i + by) for i in range(devices) if 0 <= i + by < devices]
    return lax.ppermute(shard, axis, pairs)


def transform(real_part, imag_part, count):
    span = real_part.shape[-1]
    inner = 2 * span // 128
    lead = real_part.shape[:-1]
    first = jnp.arange(64, dtype=jnp.float32)[:, None]
    middle = jnp.arange(128, dtype=jnp.float32)[None, :]
    angle_one = 2.0 * math.pi / 128.0 * jnp.mod(first * middle, 128.0)
    cos_one = jnp.cos(angle_one)
    sin_one = -jnp.sin(angle_one)
    second = jnp.arange(inner, dtype=jnp.float32)[:, None]
    angle_turn = 2.0 * math.pi / (128.0 * inner) * jnp.mod(second * middle, 128.0 * inner)
    cos_turn = jnp.cos(angle_turn)
    sin_turn = -jnp.sin(angle_turn)
    outer = jnp.arange(count // 128, dtype=jnp.float32)[None, :]
    angle_two = 2.0 * math.pi / inner * jnp.mod(second * outer, float(inner))
    cos_two = jnp.cos(angle_two)
    sin_two = -jnp.sin(angle_two)
    grid = real_part.reshape(lead + (64, inner))
    section_re = jnp.einsum("...an,ak->...nk", grid, cos_one, precision=exact)
    section_im = jnp.einsum("...an,ak->...nk", grid, sin_one, precision=exact)
    if imag_part is not None:
        grid_im = imag_part.reshape(lead + (64, inner))
        section_re = section_re - jnp.einsum("...an,ak->...nk", grid_im, sin_one, precision=exact)
        section_im = section_im + jnp.einsum("...an,ak->...nk", grid_im, cos_one, precision=exact)
    turned_re = section_re * cos_turn - section_im * sin_turn
    turned_im = section_re * sin_turn + section_im * cos_turn
    out_re = jnp.einsum("...nk,nm->...mk", turned_re, cos_two, precision=exact) - jnp.einsum(
        "...nk,nm->...mk", turned_im, sin_two, precision=exact
    )
    out_im = jnp.einsum("...nk,nm->...mk", turned_re, sin_two, precision=exact) + jnp.einsum(
        "...nk,nm->...mk", turned_im, cos_two, precision=exact
    )
    return (out_re.reshape(lead + (count,)), out_im.reshape(lead + (count,)))


def filtered(samples, filters):
    channels = samples.shape[0]
    frames = samples.shape[1] // FR
    signal = samples.astype(jnp.float32).reshape(channels, frames, FR)
    freq_re, freq_im = transform(signal, None, FR)
    padded_taps = jnp.pad(filters.astype(jnp.float32), ((0, 0), (0, FR - filters.shape[1])))
    resp_re, resp_im = transform(padded_taps, None, FR)
    resp_re = resp_re[:, None, :]
    resp_im = resp_im[:, None, :]
    spec_re = (freq_re * resp_re - freq_im * resp_im).astype(jnp.bfloat16)
    spec_im = (freq_re * resp_im + freq_im * resp_re).astype(jnp.bfloat16)
    return (spec_re, spec_im)


def body(traces, taps, bin_ids, owners):
    channels = traces.shape[0]
    frames = traces.shape[1] // FR
    spec_re, spec_im = filtered(traces, taps)
    mine = lax.axis_index("chan")
    near_re = spec_re.astype(jnp.float32)
    near_im = spec_im.astype(jnp.float32)
    results = []
    for offset in range(ROUNDS):
        far_re, far_im = passed_along((spec_re, spec_im), "chan", offset + 1)
        far_re = far_re.astype(jnp.float32)
        far_im = far_im.astype(jnp.float32)
        cross_re = jnp.sum(far_re * near_re + far_im * near_im, axis=(0, 1))
        cross_im = jnp.sum(far_im * near_re - far_re * near_im, axis=(0, 1))
        results.append(jnp.stack([cross_re, cross_im]))
    contrib = jnp.stack(results)
    nbins = owners.shape[0]
    own_bins = bin_ids[:, 0]
    labels = jnp.arange(nbins, dtype=jnp.int32)
    places = jnp.sum(jnp.where(own_bins[:, None] == labels[None, :], owners[None, :], 0), axis=1)
    valid = jnp.arange(ROUNDS, dtype=jnp.int32) < mine
    places = jnp.where(valid, places, -1)
    width = contrib.shape[2]
    flat = contrib.reshape(ROUNDS, 2 * width)
    per_device = nbins // lax.axis_size("chan")
    rows = jnp.arange(lax.axis_size("chan") * per_device, dtype=jnp.int32)
    onehot = (places[None, :] == rows[:, None]).astype(jnp.float32)
    stacked = lax.psum_scatter(
        jnp.dot(onehot, flat, precision=exact, preferred_element_type=jnp.float32),
        "chan",
        scatter_dimension=0,
        tiled=True,
    )
    stacked = stacked.reshape(per_device, 2, width)
    final = lax.psum_scatter(stacked, "hour", scatter_dimension=0, tiled=True)
    weights = jnp.where(jnp.arange(FR) == 0, 1.0, 2.0).astype(jnp.float32)
    wave_re, wave_im = transform(final[:, 0] * weights, -final[:, 1] * weights, 2 * FR)
    norm = 1.0 / (FR * math.sqrt(FR * lax.axis_size("hour") * frames * channels))
    return wave_re * norm


def solution(mesh):
    placed = (P("chan", "hour"), P("chan", None), P(None, "chan"), P())
    return jax.shard_map(
        body, mesh=mesh, in_specs=placed, out_specs=P(("chan", "hour"), None), check_vma=False
    )
```

profile of v0, /device:TPU:0, one launch (start us, length us, event | category | flops | bytes accessed | tf_op | source)
XLA Modules:
  0.0 510.1 jit_solution(9141958855128919409)
XLA Ops:
  8.3 4.0 fusion.23
  12.3 4.0 fusion.25
  18.8 10.4 %multiply_add_fusion = (f32[128,64,128]{0,2,1:T(8,128)}, f32[128,64,128]{0,2,1:T(8,128)}, f32[128,64,128]{0,2,1:T(8,128)}, f32[128,64,128]{0,2,1:T(8,128)}) fusion(f32[128,64,128]{0,2,1:T(8,128)S(1)} %fusion.21, f32[64,128]{1,0:T(8,128)S(1)} %get-tuple-element.29, f32[64,128]{1,0:T(8,128)S(1)} %get-tuple-element.30, f32[128,128,64]{1,0,2:T(8,128)S(1)} %copy-done.4, ...), kind=kOutput, calls=%fused_computation.22 | convolution fusion | flops 817963008 | bytes 30474240 | tf_op jit(solution)/shard_map/...an,ak->...nk/dot_general | solution.py:40
  29.1 5.4 %copy.65 = f32[128,64,128]{2,1,0:T(8,128)} copy(f32[128,64,128]{0,2,1:T(8,128)} %get-tuple-element.22) | data formatting | bytes 8388608 | tf_op jit(solution)/shard_map/sub | solution.py:45
  34.5 4.4 fusion.75
  42.4 5.4 %copy.58 = f32[128,64,128]{2,1,0:T(8,128)} copy(f32[128,64,128]{0,2,1:T(8,128)} %get-tuple-element.27) | data formatting | bytes 8388608 | tf_op jit(solution)/shard_map/sub | solution.py:45
  47.8 5.9 %fusion.77 = f32[32,128,128]{2,0,1:T(8,128)} fusion(f32[128,64,128]{2,1,0:T(8,128)} %copy.58), kind=kOutput, calls=%fused_computation.119 | convolution fusion | flops 402671616 | bytes 6291456 | tf_op jit(solution)/shard_map/...nk,nm->...mk/dot_general | solution.py:50
  57.2 5.4 %copy.68 = f32[128,64,128]{2,1,0:T(8,128)} copy(f32[128,64,128]{0,2,1:T(8,128)} %get-tuple-element.21) | data formatting | bytes 8388608 | tf_op jit(solution)/shard_map/add | solution.py:46
  62.6 6.5 %subtract_bitcast_fusion = f32[128,32,128]{2,1,0:T(8,128)} fusion(f32[32,128,128]{2,0,1:T(8,128)} %fusion.83, f32[128,64,128]{2,1,0:T(8,128)} %copy.68), kind=kOutput, calls=%fused_computation.44 | convolution fusion | flops 403195904 | bytes 8388608 | tf_op jit(solution)/shard_map/...nk,nm->...mk/dot_general | solution.py:47
  77.1 5.4 %copy.59 = f32[128,64,128]{2,1,0:T(8,128)} copy(f32[128,64,128]{0,2,1:T(8,128)} %get-tuple-element.28) | data formatting | bytes 8388608 | tf_op jit(solution)/shard_map/add | solution.py:46
  82.5 6.5 %add_bitcast_fusion.1 = f32[128,1,32,128]{3,2,0,1:T(8,128)} fusion(f32[32,128,128]{2,0,1:T(8,128)} %fusion.77, f32[128,64,128]{2,1,0:T(8,128)} %copy.59), kind=kOutput, calls=%fused_computation.43 | convolution fusion | flops 403193856 | bytes 8388608 | tf_op jit(solution)/shard_map/...nk,nm->...mk/dot_general | solution.py:50
  89.0 3.6 subtract_bitcast_fusion.1
  98.1 4.7 add_convert_fusion
  102.8 6.0 %collective-permute-start.7 = (bf16[128,1,4096]{2,0,1:T(8,128)(2,1)S(1)}, bf16[128,1,4096]{2,0,1:T(8,128)(2,1)S(1)}, u32[]{:S(2)}, u32[]{:S(2)}) collective-permute-start(bf16[128,1,4096]{2,0,1:T(8,128)(2,1)S(1)} %get-tuple-element.25), channel_id=1, source_target_pairs={{0,16},{4,20},{8,24},{12,28},{1,17},{5,21},{9,25},{13,29},{2,18},{... | collective-permute-start | bytes 3145736 | tf_op jit(solution)/shard_map/ppermute | solution.py:18
  108.8 4.5 collective-permute-start.5
  114.7 4.3 collective-permute-start.1
  121.3 11.1 %collective-permute-done.7 = bf16[128,1,4096]{2,0,1:T(8,128)(2,1)S(1)} collective-permute-done((bf16[128,1,4096]{2,0,1:T(8,128)(2,1)S(1)}, bf16[128,1,4096]{2,0,1:T(8,128)(2,1)S(1)}, u32[]{:S(2)}, u32[]{:S(2)}) %collective-permute-start.7) | collective-permute-done | bytes 1048608 | tf_op jit(solution)/shard_map/ppermute | solution.py:18
  132.3 49.2 %collective-permute-start.4 = (bf16[128,1,4096]{2,0,1:T(8,128)(2,1)}, bf16[128,1,4096]{2,0,1:T(8,128)(2,1)}, u32[]{:S(2)}, u32[]{:S(2)}) collective-permute-start(bf16[128,1,4096]{2,0,1:T(8,128)(2,1)} %get-tuple-element.26), channel_id=1, source_target_pairs={{0,12},{4,16},{8,20},{12,24},{16,28},{1,13},{5,17},{9,21},{13,25},... | collective-permute-start | bytes 3145736 | tf_op jit(solution)/shard_map/ppermute | solution.py:18
  184.8 24.5 %collective-permute-start = (bf16[128,1,4096]{2,0,1:T(8,128)(2,1)}, bf16[128,1,4096]{2,0,1:T(8,128)(2,1)}, u32[]{:S(2)}, u32[]{:S(2)}) collective-permute-start(bf16[128,1,4096]{2,0,1:T(8,128)(2,1)} %get-tuple-element.26), channel_id=1, source_target_pairs={{0,4},{4,8},{8,12},{12,16},{16,20},{20,24},{24,28},{1,5},{5,9},{9,... | collective-permute-start | bytes 3145736 | tf_op jit(solution)/shard_map/ppermute | solution.py:18
  209.5 12.9 %collective-permute-done.4 = bf16[128,1,4096]{2,0,1:T(8,128)(2,1)} collective-permute-done((bf16[128,1,4096]{2,0,1:T(8,128)(2,1)}, bf16[128,1,4096]{2,0,1:T(8,128)(2,1)}, u32[]{:S(2)}, u32[]{:S(2)}) %collective-permute-start.4) | collective-permute-done | bytes 1048608 | tf_op jit(solution)/shard_map/ppermute | solution.py:18
  222.4 21.3 %collective-permute-done.2 = bf16[128,1,4096]{2,0,1:T(8,128)(2,1)} collective-permute-done((bf16[128,1,4096]{2,0,1:T(8,128)(2,1)}, bf16[128,1,4096]{2,0,1:T(8,128)(2,1)}, u32[]{:S(2)}, u32[]{:S(2)}) %collective-permute-start.2) | collective-permute-done | bytes 1048608 | tf_op jit(solution)/shard_map/ppermute | solution.py:18
  243.7 5.3 %fusion.3 = (f32[4096]{0:T(1024)S(1)}, f32[4096]{0:T(1024)S(1)}, f32[4096]{0:T(1024)S(1)}, f32[4096]{0:T(1024)S(1)}, f32[4096]{0:T(1024)S(1)}, /*index=5*/f32[4096]{0:T(1024)S(1)}, f32[4096]{0:T(1024)S(1)}, f32[4096]{0:T(1024)S(1)}) fusion(bf16[128,1,4096]{2,0,1:T(8,128)(2,1)} %get-tuple-element.26, bf16[128,1,4096]{2,0,1:T(8,128)(2,1)} %collective-permute-done, ...), kind=kLoop, calls=%fused_computation.25 | loop fusion | flops 21987328 | bytes 10616832 | tf_op jit(solution)/shard_map/reduce_sum | solution.py:82
  252.4 212.9 %all-reduce.6.cloned.1.call-done = f32[32,8192]{1,0:T(8,128)} async-done(((f32[32,8192]{1,0:T(8,128)}), f32[32,8192]{1,0:T(8,128)}) %all-reduce.6.cloned.1.call-update) | async-done | bytes 1048592
  467.7 31.0 %all-reduce.8.cloned.1.call-done = f32[4,2,4096]{2,1,0:T(2,128)} async-done(((f32[4,2,4096]{2,1,0:T(2,128)}), f32[4,2,4096]{2,1,0:T(2,128)}) %all-reduce.8.cloned.1.call-update) | async-done | bytes 131088
  (72 shorter events, 41.2 us)
Async XLA Ops:
  6.5 458.8 %all-reduce.6.cloned.1.call-start = ((), (), s32[]{:S(2)}) async-start(), calls=%async_computation | async-start | bytes 2097152
  12.3 4.0 copy-start.7
  16.6 2.2 copy-start.4
  34.5 4.4 copy-start.2
  47.8 5.9 %copy-start.3 = (f32[128,64,128]{2,1,0:T(8,128)S(1)}, f32[128,64,128]{2,1,0:T(8,128)}, u32[]{:S(2)}) copy-start(f32[128,64,128]{2,1,0:T(8,128)} %copy.58) | copy-start | bytes 12582916
  62.6 6.5 %copy-start = (f32[128,64,128]{2,1,0:T(8,128)S(1)}, f32[128,64,128]{2,1,0:T(8,128)}, u32[]{:S(2)}) copy-start(f32[128,64,128]{2,1,0:T(8,128)} %copy.68) | copy-start | bytes 12582916
  82.5 6.5 %copy-start.1 = (f32[128,64,128]{2,1,0:T(8,128)S(1)}, f32[128,64,128]{2,1,0:T(8,128)}, u32[]{:S(2)}) copy-start(f32[128,64,128]{2,1,0:T(8,128)} %copy.59) | copy-start | bytes 12582916
  82.5 6.5 %copy-start.5 = (f32[32,128,128]{2,0,1:T(8,128)S(1)}, f32[32,128,128]{2,0,1:T(8,128)}, u32[]{:S(2)}) copy-start(f32[32,128,128]{2,0,1:T(8,128)} %fusion.85) | copy-start | bytes 6291460
  98.1 111.2 %copy-start.8 = (s32[32]{0:T(128)S(1)}, s32[32]{0:T(128)}, u32[]{:S(2)}) copy-start(s32[32]{0:T(128)} %param.7) | copy-start | bytes 388
  98.1 111.2 %copy-start.9 = (s32[4,1]{0,1:T(1,128)S(1)}, s32[4,1]{0,1:T(1,128)}, u32[]{:S(2)}) copy-start(s32[4,1]{0,1:T(1,128)} %param.6) | copy-start | bytes 52
  102.8 29.5 %collective-permute-start.7 = (bf16[128,1,4096]{2,0,1:T(8,128)(2,1)S(1)}, bf16[128,1,4096]{2,0,1:T(8,128)(2,1)S(1)}, u32[]{:S(2)}, u32[]{:S(2)}) collective-permute-start(bf16[128,1,4096]{2,0,1:T(8,128)(2,1)S(1)} %get-tuple-element.25), channel_id=1, source_target_pairs={{0,16},{4,20},{8,24},{12,28},{1,17},{5,21},{9,25},{13,29},{2,18},{... | collective-permute-start | bytes 3145736 | tf_op jit(solution)/shard_map/ppermute | solution.py:18
  108.8 72.7 %collective-permute-start.5 = (bf16[128,1,4096]{2,0,1:T(8,128)(2,1)S(1)}, bf16[128,1,4096]{2,0,1:T(8,128)(2,1)S(1)}, u32[]{:S(2)}, u32[]{:S(2)}) collective-permute-start(bf16[128,1,4096]{2,0,1:T(8,128)(2,1)S(1)} %get-tuple-element.25), channel_id=1, source_target_pairs={{0,12},{4,16},{8,20},{12,24},{16,28},{1,13},{5,17},{9,21},{13,25},... | collective-permute-start | bytes 3145736 | tf_op jit(solution)/shard_map/ppermute | solution.py:18
  113.3 70.5 %collective-permute-start.3 = (bf16[128,1,4096]{2,0,1:T(8,128)(2,1)S(1)}, bf16[128,1,4096]{2,0,1:T(8,128)(2,1)S(1)}, u32[]{:S(2)}, u32[]{:S(2)}) collective-permute-start(bf16[128,1,4096]{2,0,1:T(8,128)(2,1)S(1)} %get-tuple-element.25), channel_id=1, source_target_pairs={{0,8},{4,12},{8,16},{12,20},{16,24},{20,28},{1,9},{5,13},{9,17},{1... | collective-permute-start | bytes 3145736 | tf_op jit(solution)/shard_map/ppermute | solution.py:18
  114.7 94.9 %collective-permute-start.1 = (bf16[128,1,4096]{2,0,1:T(8,128)(2,1)S(1)}, bf16[128,1,4096]{2,0,1:T(8,128)(2,1)}, u32[]{:S(2)}, u32[]{:S(2)}) collective-permute-start(bf16[128,1,4096]{2,0,1:T(8,128)(2,1)S(1)} %get-tuple-element.25), channel_id=1, source_target_pairs={{0,4},{4,8},{8,12},{12,16},{16,20},{20,24},{24,28},{1,5},{5,9},{9,... | collective-permute-start | bytes 3145736 | tf_op jit(solution)/shard_map/ppermute | solution.py:18
  119.0 90.5 %collective-permute-start.6 = (bf16[128,1,4096]{2,0,1:T(8,128)(2,1)}, bf16[128,1,4096]{2,0,1:T(8,128)(2,1)}, u32[]{:S(2)}, u32[]{:S(2)}) collective-permute-start(bf16[128,1,4096]{2,0,1:T(8,128)(2,1)} %get-tuple-element.26), channel_id=1, source_target_pairs={{0,16},{4,20},{8,24},{12,28},{1,17},{5,21},{9,25},{13,29},{2,18},{... | collective-permute-start | bytes 3145736 | tf_op jit(solution)/shard_map/ppermute | solution.py:18
  132.3 90.1 %collective-permute-start.4 = (bf16[128,1,4096]{2,0,1:T(8,128)(2,1)}, bf16[128,1,4096]{2,0,1:T(8,128)(2,1)}, u32[]{:S(2)}, u32[]{:S(2)}) collective-permute-start(bf16[128,1,4096]{2,0,1:T(8,128)(2,1)} %get-tuple-element.26), channel_id=1, source_target_pairs={{0,12},{4,16},{8,20},{12,24},{16,28},{1,13},{5,17},{9,21},{13,25},... | collective-permute-start | bytes 3145736 | tf_op jit(solution)/shard_map/ppermute | solution.py:18
  181.5 62.2 %collective-permute-start.2 = (bf16[128,1,4096]{2,0,1:T(8,128)(2,1)}, bf16[128,1,4096]{2,0,1:T(8,128)(2,1)}, u32[]{:S(2)}, u32[]{:S(2)}) collective-permute-start(bf16[128,1,4096]{2,0,1:T(8,128)(2,1)} %get-tuple-element.26), channel_id=1, source_target_pairs={{0,8},{4,12},{8,16},{12,20},{16,24},{20,28},{1,9},{5,13},{9,17},{1... | collective-permute-start | bytes 3145736 | tf_op jit(solution)/shard_map/ppermute | solution.py:18
  183.8 1.0 copy-start.6
  184.8 58.9 %collective-permute-start = (bf16[128,1,4096]{2,0,1:T(8,128)(2,1)}, bf16[128,1,4096]{2,0,1:T(8,128)(2,1)}, u32[]{:S(2)}, u32[]{:S(2)}) collective-permute-start(bf16[128,1,4096]{2,0,1:T(8,128)(2,1)} %get-tuple-element.26), channel_id=1, source_target_pairs={{0,4},{4,8},{8,12},{12,16},{16,20},{20,24},{24,28},{1,5},{5,9},{9,... | collective-permute-start | bytes 3145736 | tf_op jit(solution)/shard_map/ppermute | solution.py:18
  249.1 2.1 copy-start.11
  249.1 218.0 %copy-start.10 = (u32[32]{0:T(128)S(1)}, u32[32]{0:T(128)}, u32[]{:S(2)}) copy-start(u32[32]{0:T(128)} %constant.76) | copy-start | bytes 388
  251.1 247.6 %all-reduce.8.cloned.1.call-start = ((), (), s32[]{:S(2)}) async-start(), calls=%async_computation.1 | async-start | bytes 262144
Sparse Core Ops, SparseCore 0:
  251.2 214.0 all-reduce.5
  467.7 30.9 all-reduce.7
where the time goes:
time: 511 us; the launch traced here: 510 us
  waiting for transfers between devices  289 us (57%)
  starting transfers between devices  94.5 us (18%)
  matrix products  62.2 us (12%)
  local copies, waits for them, and re-layouts  37.8 us (7%)
  between operations  14.3 us (3%)
  other arithmetic  12.1 us (2%)
    unnamed x4, waiting for transfers between devices  244 us
    ppermute x8, starting transfers between devices, passed_along(): return lax.ppermute(shard, axis, pairs)  94.5 us
    ppermute x8, waiting for transfers between devices, passed_along(): return lax.ppermute(shard, axis, pairs)  45.3 us
    dot_general x3, matrix products, transform(): section_im = jnp.einsum('...an,ak->...nk', grid, sin_one, precision=exact)  14.7 us
    dot_general x3, matrix products, transform(): jnp.einsum('...nk,nm->...mk', turned_im, sin_two, precision=exact)  11.1 us
    add x2, local copies, waits for them, and re-layouts, transform(): turned_im = section_re * sin_turn + section_im * cos_turn  10.8 us
    sub x2, local copies, waits for them, and re-layouts, transform(): turned_re = section_re * cos_turn - section_im * sin_turn  10.8 us
    dot_general x2, matrix products, transform(): jnp.einsum('...nk,nm->...mk', turned_re, sin_two, precision=exact)  10.3 us
  transfers between devices with their start and end apart: 10, of which 5 were waited for; matrix products, arithmetic and copies ran while one was open for 0% of the time, Pallas kernels for 0%

commit v1 on v0

--- a/solution.py
+++ b/solution.py
@@ -1,16 +1,20 @@
+import functools
 import math
 
 import jax
 import jax.numpy as jnp
+import numpy as np
 from jax import lax
+from jax.experimental import pallas as pl
+from jax.experimental.pallas import tpu as pltpu
 from jax.sharding import PartitionSpec as P
 
 FR = 4096
 ROUNDS = 4
+MESH = pl.DeviceIdType.MESH
 
 
 exact = lax.Precision.HIGHEST
-
 
 def passed_along(shard, axis, by):
     devices = lax.axis_size(axis)
@@ -107,9 +111,318 @@
     norm = 1.0 / (FR * math.sqrt(FR * lax.axis_size("hour") * frames * channels))
     return wave_re * norm
 
+SPLIT = 8
+SUB = FR // SPLIT
+LANES = 128
+TILES = SUB // LANES
+
+
+def sub_tables():
+    a = np.arange(SUB)[:, None]
+    k1 = np.arange(SUB)[None, :]
+    turn = 2.0 * np.pi * ((a * k1) % (2 * SUB)) / (2 * SUB)
+    cos, sin = np.cos(turn), -np.sin(turn)
+    sin[:, 0] = 1.0 - 2.0 * (np.arange(SUB) % 2)
+    table = np.stack([cos.reshape(SUB, TILES, LANES), sin.reshape(SUB, TILES, LANES)], axis=2)
+    return table.reshape(SUB, 2 * SUB)
+
+
+def two_parts(table):
+    high = table.astype(jnp.bfloat16)
+    low = (table - high.astype(np.float64)).astype(jnp.bfloat16)
+    return high, low
+
+
+def pick_table():
+    span = SPLIT * LANES
+    table = np.zeros((span, span), np.float32)
+    for n in range(SPLIT):
+        for b in range(LANES):
+            table[SPLIT * b + n, n * LANES + b] = 1.0
+    return table.astype(jnp.bfloat16)
+
+
+def turn_table():
+    n = np.arange(SPLIT)[:, None]
+    k1 = np.arange(SUB)[None, :]
+    turn = 2.0 * np.pi * n * k1 / (2 * FR)
+    table = np.stack([np.cos(turn), -np.sin(turn)], axis=1).reshape(SPLIT, 2, TILES, 1, LANES)
+    table = np.broadcast_to(table.transpose(2, 0, 1, 3, 4), (TILES, SPLIT, 2, 8, LANES))
+    return np.ascontiguousarray(table).astype(np.float32)
+
+
+def times(value, angle):
+    re, im = value
+    c, s = math.cos(angle), math.sin(angle)
+    if abs(s) < 1e-12:
+        return (re, im) if c > 0 else (-re, -im)
+    if abs(c) < 1e-12:
+        return (-im, re) if s > 0 else (im, -re)
+    if abs(abs(c) - abs(s)) < 1e-12:
+        root = abs(c)
+        p, q = math.copysign(1.0, c), math.copysign(1.0, s)
+        first = (re if p > 0 else -re) + (-im if q > 0 else im)
+        second = (re if q > 0 else -re) + (im if p > 0 else -im)
+        return first * root, second * root
+    return re * c - im * s, re * s + im * c
+
+
+def small_dft(values, sign, half=False):
+    size = len(values)
+    if size == 1:
+        return values
+    even = small_dft(values[0::2], sign)
+    odd = small_dft(values[1::2], sign)
+    low, high = [], []
+    for k in range(size // 2):
+        turned = times(odd[k], sign * 2.0 * math.pi * k / size)
+        low.append((even[k][0] + turned[0], even[k][1] + turned[1]))
+        if not half:
+            high.append((even[k][0] - turned[0], even[k][1] - turned[1]))
+    return low + high
+
+
+def pairs_of(blocks):
+    return [(r, i) for r in range(ROUNDS) for i in range(blocks) if i >= r + 1]
+
+
+def correlate_kernel(blocks, x, taps, pick, high, low, turns, onehot, out, xd, td, fx, fh, spec, cross):
+    rows = x.shape[0]
+    per = rows // blocks
+    span = SPLIT * LANES
+    for q in range(FR // span):
+        part = jnp.dot(
+            x[:, q * span : (q + 1) * span], pick[...], preferred_element_type=jnp.float32
+        ).astype(jnp.bfloat16)
+        for n in range(SPLIT):
+            xd[n, :, q * LANES : (q + 1) * LANES] = part[:, n * LANES : (n + 1) * LANES]
+    count = taps.shape[1]
+    part = jnp.dot(taps[...], pick[:count, :], preferred_element_type=jnp.float32).astype(jnp.bfloat16)
+    for n in range(SPLIT):
+        td[n] = part[:, n * LANES : (n + 1) * LANES]
+
+    @pl.loop(0, SPLIT)
+    def _(n):
+        fx[n] = jnp.dot(xd[n], high[...], preferred_element_type=jnp.float32) + jnp.dot(
+            xd[n], low[...], preferred_element_type=jnp.float32
+        )
+        fh[n] = jnp.dot(td[n], high[:LANES, :], preferred_element_type=jnp.float32) + jnp.dot(
+            td[n], low[:LANES, :], preferred_element_type=jnp.float32
+        )
+
+    pairs = pairs_of(blocks)
+    lane0 = lax.broadcasted_iota(jnp.int32, (8, LANES), 1) == 0
+    for t in range(TILES):
+
+        @pl.loop(0, rows // 8)
+        def _(g):
+            here = pl.ds(pl.multiple_of(8 * g, 8), 8)
+
+            def bins_of(f):
+                values, extra = [], []
+                for n in range(SPLIT):
+                    re = f[n, here, 2 * t * LANES : (2 * t + 1) * LANES]
+                    im = f[n, here, (2 * t + 1) * LANES : (2 * t + 2) * LANES]
+                    if t == 0:
+                        angle = -math.pi * n / SPLIT
+                        extra.append((im * math.cos(angle), im * math.sin(angle)))
+                        im = jnp.where(lane0, 0.0, im)
+                    if n == 0:
+                        values.append((re, im))
+                    else:
+                        c, s = turns[t, n, 0], turns[t, n, 1]
+                        values.append((re * c - im * s, re * s + im * c))
+                found = small_dft(values, -1)
+                if t == 0:
+                    more = small_dft(extra, -1, half=True)
+                    for k2 in range(SPLIT // 2):
+                        old = found[SPLIT // 2 + k2]
+                        found[SPLIT // 2 + k2] = tuple(
+                            jnp.where(lane0, more[k2][z], old[z]) for z in range(2)
+                        )
+                return found
+
+            freq = bins_of(fx)
+            resp = bins_of(fh)
+            for k2 in range(SPLIT):
+                (xr, xi), (hr, hi) = freq[k2], resp[k2]
+                spec[k2, 0, here, :] = (xr * hr - xi * hi).astype(jnp.bfloat16).astype(jnp.float32)
+                spec[k2, 1, here, :] = (xr * hi + xi * hr).astype(jnp.bfloat16).astype(jnp.float32)
+
+        @pl.loop(0, SPLIT)
+        def _(k2):
+            for p, (r, i) in enumerate(pairs):
+                re = im = None
+                for c in range(per // 8):
+                    near = pl.ds(i * per + 8 * c, 8)
+                    far = pl.ds((i - r - 1) * per + 8 * c, 8)
+                    nr, ni = spec[k2, 0, near, :], spec[k2, 1, near, :]
+                    fr, fi = spec[k2, 0, far, :], spec[k2, 1, far, :]
+                    one, two = fr * nr + fi * ni, fi * nr - fr * ni
+                    re, im = (one, two) if re is None else (re + one, im + two)
+                cross[8 * p : 8 * p + 8, :LANES] = re
+                cross[8 * p : 8 * p + 8, LANES:] = im
+            total = cross[...]
+            top = total.astype(jnp.bfloat16)
+            rest = (total - top.astype(jnp.float32)).astype(jnp.bfloat16)
+            place = pl.multiple_of((t * SPLIT + k2) * 2 * LANES, 2 * LANES)
+            out[:, pl.ds(place, 2 * LANES)] = jnp.dot(
+                onehot[...], top, preferred_element_type=jnp.float32
+            ) + jnp.dot(onehot[...], rest, preferred_element_type=jnp.float32)
+
+
+def correlate(x, taps, onehot, blocks):
+    rows = x.shape[0]
+    high, low = two_parts(sub_tables())
+    nbins, depth = onehot.shape
+    vmem = pl.BlockSpec(memory_space=pltpu.VMEM)
+    return pl.pallas_call(
+        functools.partial(correlate_kernel, blocks),
+        out_shape=jax.ShapeDtypeStruct((nbins, 2 * FR), jnp.float32),
+        in_specs=[vmem] * 7,
+        out_specs=vmem,
+        scratch_shapes=[
+            pltpu.VMEM((SPLIT, rows, SUB), jnp.bfloat16),
+            pltpu.VMEM((SPLIT, rows, LANES), jnp.bfloat16),
+            pltpu.VMEM((SPLIT, rows, 2 * SUB), jnp.float32),
+            pltpu.VMEM((SPLIT, rows, 2 * SUB), jnp.float32),
+            pltpu.VMEM((SPLIT, 2, rows, LANES), jnp.float32),
+            pltpu.VMEM((depth, 2 * LANES), jnp.float32),
+        ],
+        compiler_params=pltpu.CompilerParams(vmem_limit_bytes=48 * 2**20),
+    )(x, taps, jnp.asarray(pick_table()), jnp.asarray(high), jnp.asarray(low), jnp.asarray(turn_table()), onehot)
+
+
+def wave_of(row, norm):
+    tiles = row.reshape(TILES, SPLIT, 2, LANES).transpose(2, 1, 0, 3).reshape(2, SPLIT, SUB)
+    weight = np.full((SPLIT, SUB), 2.0)
+    weight[0, 0] = 1.0
+    tiles = tiles * jnp.asarray(weight.astype(np.float32) * np.float32(norm))
+    main = np.ones((SPLIT, SUB))
+    main[SPLIT // 2 :, 0] = 0.0
+    re, im = tiles[0] * main.astype(np.float32), tiles[1] * main.astype(np.float32)
+    got = small_dft([(re[k], im[k]) for k in range(SPLIT)], 1)
+    g_re = jnp.stack([v[0] for v in got])
+    g_im = jnp.stack([v[1] for v in got])
+    turn = 2.0 * np.pi * np.arange(SPLIT)[:, None] * np.arange(SUB)[None, :] / (2 * FR)
+    c, s = np.cos(turn).astype(np.float32), np.sin(turn).astype(np.float32)
+    y_re = g_re * c - g_im * s
+    y_im = g_re * s + g_im * c
+    l2 = np.arange(SPLIT)[:, None]
+    k2 = np.arange(SPLIT // 2)[None, :]
+    angle = 2.0 * np.pi * (k2 * l2 / SPLIT + l2 / (2 * SPLIT))
+    extra = jnp.sum(
+        np.cos(angle).astype(np.float32) * tiles[0, SPLIT // 2 :, 0][None, :]
+        - np.sin(angle).astype(np.float32) * tiles[1, SPLIT // 2 :, 0][None, :],
+        axis=1,
+    )
+    y_im = jnp.where(jnp.arange(SUB)[None, :] == 0, extra[:, None], y_im)
+    l1 = np.arange(2 * SUB)[None, :]
+    k1 = np.arange(SUB)[:, None]
+    turn = 2.0 * np.pi * ((k1 * l1) % (2 * SUB)) / (2 * SUB)
+    cos, sin = np.cos(turn), -np.sin(turn)
+    sin[0, :] = 1.0 - 2.0 * (np.arange(2 * SUB) % 2)
+    table = np.concatenate([cos, sin]).astype(np.float32)
+    wave = jnp.dot(jnp.concatenate([y_re, y_im], axis=1), jnp.asarray(table), precision=exact)
+    return wave.T.reshape(1, 2 * FR)
+
+
+def exchange_kernel(blocks, x, taps, ids, x_out, taps_out, ids_out, send, recv, keep):
+    me = lax.axis_index("chan")
+    barrier = pltpu.get_barrier_semaphore()
+    for o in range(1, blocks):
+        pl.semaphore_signal(
+            barrier, inc=1, device_id={"chan": lax.rem(me + o, blocks)}, device_id_type=MESH
+        )
+    pl.semaphore_wait(barrier, blocks - 1)
+    copies = []
+    for o in range(1, blocks):
+        to = lax.rem(me + o, blocks)
+        for z, (src, dst) in enumerate(((ids, ids_out), (taps.at[to], taps_out), (x.at[to], x_out))):
+            copy = pltpu.make_async_remote_copy(
+                src_ref=src,
+                dst_ref=dst.at[me],
+                send_sem=send.at[z, o],
+                recv_sem=recv.at[z, o],
+                device_id={"chan": to},
+                device_id_type=MESH,
+            )
+            copy.start()
+            copies.append(copy)
+    mine = []
+    for z, (src, dst) in enumerate(((ids, ids_out), (taps.at[me], taps_out), (x.at[me], x_out))):
+        copy = pltpu.make_async_copy(src, dst.at[me], keep.at[z])
+        copy.start()
+        mine.append(copy)
+    for copy in mine:
+        copy.wait()
+    for copy in copies:
+        copy.wait()
+
+
+def exchange(x, taps, ids, blocks):
+    hbm = pl.BlockSpec(memory_space=pl.ANY)
+    return pl.pallas_call(
+        functools.partial(exchange_kernel, blocks),
+        out_shape=(
+            jax.ShapeDtypeStruct(x.shape, x.dtype),
+            jax.ShapeDtypeStruct(taps.shape, taps.dtype),
+            jax.ShapeDtypeStruct((blocks,) + ids.shape, ids.dtype),
+        ),
+        in_specs=[hbm] * 3,
+        out_specs=(hbm,) * 3,
+        scratch_shapes=[
+            pltpu.SemaphoreType.DMA((3, blocks)),
+            pltpu.SemaphoreType.DMA((3, blocks)),
+            pltpu.SemaphoreType.DMA((3,)),
+        ],
+        compiler_params=pltpu.CompilerParams(collective_id=0, has_side_effects=True),
+    )(x, taps, ids)
+
+
+def onehot_of(all_ids, owners, blocks):
+    pairs = pairs_of(blocks)
+    flat = jnp.stack([all_ids[r, i] for r, i in pairs])
+    nbins = owners.shape[0]
+    labels = jnp.arange(nbins, dtype=jnp.int32)
+    places = jnp.sum(jnp.where(flat[:, None] == labels[None, :], owners[None, :], 0), axis=1)
+    hot = (places[None, :] == labels[:, None]).astype(jnp.bfloat16)
+    return jnp.repeat(hot, 8, axis=1)
+
+
+def split_body(traces, taps, bin_ids, owners):
+    blocks = lax.axis_size("chan")
+    channels = traces.shape[0]
+    per = channels // blocks
+    ids = jnp.broadcast_to(jnp.pad(bin_ids, ((0, 8 - ROUNDS), (0, 0))), (8, LANES))
+    x, filters, all_ids = exchange(
+        traces.reshape(blocks, per, FR), taps.reshape(blocks, per, taps.shape[1]), ids, blocks
+    )
+    onehot = onehot_of(all_ids[:, :ROUNDS, 0].T, owners, blocks)
+    stack = correlate(x.reshape(channels, FR), filters.reshape(channels, taps.shape[1]), onehot, blocks)
+    final = lax.psum_scatter(stack, ("chan", "hour"), scatter_dimension=0, tiled=True)
+    norm = 1.0 / (FR * math.sqrt(FR * lax.axis_size("hour") * channels))
+    return wave_of(final[0], norm)
+
 
 def solution(mesh):
     placed = (P("chan", "hour"), P("chan", None), P(None, "chan"), P())
-    return jax.shard_map(
-        body, mesh=mesh, in_specs=placed, out_specs=P(("chan", "hour"), None), check_vma=False
-    )
+
+    def whole(traces, taps, bin_ids, owners):
+        chan, hour = mesh.shape["chan"], mesh.shape["hour"]
+        channels = traces.shape[0] // chan
+        fits = (
+            channels % (16 * chan) == 0
+            and traces.shape[1] == hour * FR
+            and taps.shape[1] == SPLIT * LANES // 2
+            and owners.shape[0] == chan * hour
+        )
+        return jax.shard_map(
+            split_body if fits else body,
+            mesh=mesh,
+            in_specs=placed,
+            out_specs=P(("chan", "hour"), None),
+            check_vma=False,
+        )(traces, taps, bin_ids, owners)
+
+    return whole

time: 511 us -> 229 us (0.45)
  waiting for transfers between devices: 289 us -> 138 us
  starting transfers between devices: 94.5 us -> 0.01 us
  matrix products: 62.2 us -> 3.8 us
  Pallas kernels: 0 us -> 44.3 us
  local copies, waits for them, and re-layouts: 37.8 us -> 24.3 us
  other arithmetic: 12.1 us -> 5.21 us
    unnamed x4 -> x2, waiting for transfers between devices: 244 us -> 138 us
    ppermute x8 -> x0, starting transfers between devices: 94.5 us -> none  [passed_along(): return lax.ppermute(shard, axis, pairs)]
    dot_general x19 -> x2, matrix products: 62.2 us -> 3.8 us  [wave_of(): jnp.dot(jnp.concatenate([y_re, y_im], axis=1), jnp.asarray(table), precis...]
    ppermute x8 -> x0, waiting for transfers between devices: 45.3 us -> none  [passed_along(): return lax.ppermute(shard, axis, pairs)]
    pallas_call x0 -> x2, Pallas kernels: none -> 44.3 us  [the longest x1 26.3 us: exchange(): pl.pallas_call(functools.partial(exchange_kernel, blocks), out_shape=(jax...]
    add x2 -> x0, local copies, waits for them, and re-layouts: 10.8 us -> none  [transform(): turned_im = section_re * sin_turn + section_im * cos_turn]
    sub x2 -> x0, local copies, waits for them, and re-layouts: 10.8 us -> none  [transform(): turned_re = section_re * cos_turn - section_im * sin_turn]
    another operation x2 -> x3, local copies, waits for them, and re-layouts: 4.5 us -> 13.9 us  [the longest x1 13.8 us: onehot_of(): flat = jnp.stack([all_ids[r, i] for r, i in pairs])]
  transfers between devices with their start and end apart: 10 -> 1, of which waited for: 5 -> 1; matrix products, arithmetic and copies ran while one was open for 0% -> 0% of each run, Pallas kernels for 0% -> 0%
where the time goes in v1:
time: 229 us
  waiting for transfers between devices  138 us (60%)
  Pallas kernels  44.3 us (19%)
  local copies, waits for them, and re-layouts  24.3 us (11%)
  between operations  13.6 us (6%)
  other arithmetic  5.21 us (2%)
  matrix products  3.8 us (2%)
    unnamed x2, waiting for transfers between devices  138 us
    pallas_call x1, Pallas kernels, exchange(): pl.pallas_call(functools.partial(exchange_kernel, blocks), out_shape=(jax...  26.3 us
    pallas_call x1, Pallas kernels, correlate(): pl.pallas_call(functools.partial(correlate_kernel, blocks), out_shape=jax...  18 us
    another operation x1, local copies, waits for them, and re-layouts, onehot_of(): flat = jnp.stack([all_ids[r, i] for r, i in pairs])  13.8 us
    unnamed x25, local copies, waits for them, and re-layouts  5.32 us
  transfers between devices with their start and end apart: 1, of which 1 were waited for; matrix products, arithmetic and copies ran while one was open for 0% of the time, Pallas kernels for 0%

profile of v1, /device:TPU:0, one launch (start us, length us, event | category | flops | bytes accessed | tf_op | source)
XLA Modules:
  0.0 228.7 jit_solution(1602691202064662022)
XLA Ops:
  6.5 0.7 pad_bitcast_fusion
  7.3 0.7 broadcast_in_dim.47.ids
  8.0 26.3 %shard_map.154 = (bf16[8,16,4096]{2,1,0:T(8,128)(2,1)}, bf16[8,16,512]{2,1,0:T(8,128)(2,1)}, s32[8,8,128]{2,1,0:T(8,128)}) custom-call(bf16[8,16,4096]{2,1,0:T(8,128)(2,1)} %bitcast.64, bf16[8,16,512]{2,1,0:T(8,128)(2,1)} %bitcast.65, s32[8,128]{1,0:T(8,128)} %broadcast_in_dim.47.ids), custom_call_target="tpu_custom_call" | custom-call | tf_op jit(solution)/shard_map/pallas_call | solution.py:365
  34.2 0.8 slice.129
  35.1 0.7 fusion.15
  35.8 0.6 fusion.16
  36.5 13.8 %stack.6 = s32[22]{0:T(128)S(1)} concatenate(s32[1]{0:T(128)} %bitcast.7, s32[1]{0:T(128)} %bitcast.9, s32[1]{0:T(128)} %bitcast.10, s32[1]{0:T(128)} %bitcast.11, s32[1]{0:T(128)} %bitcast.12, s32[1]{0:T(128)} %bitcast.13, s32[1]{0:T(128)} %bitcast.14, s32[1]{0:T(128)} %bitcast.15, s32[1]{0:T(128)} %bitcast.16, s32[1]{0:T(128)} %bitcast.17, s32[1]{0:T(128)} %bitcast.18, ...), dimensions={0} | concatenate | bytes 176 | tf_op jit(solution)/shard_map/stack | solution.py:385
  50.3 0.8 select_reduce_fusion
  51.3 1.2 copy-done.1
  52.5 1.2 copy-done.2
  53.8 0.9 copy-done.3
  54.7 0.9 copy-done.4
  55.6 18.0 %shard_map.155 = f32[32,8192]{1,0:T(8,128)} custom-call(bf16[128,4096]{1,0:T(8,128)(2,1)S(1)} %bitcast.62, bf16[128,512]{1,0:T(8,128)(2,1)S(1)} %bitcast.63, bf16[1024,1024]{1,0:T(8,128)(2,1)} %constant.13.clone.pick, bf16[512,1024]{1,0:T(8,128)(2,1)S(1)} %copy-done, bf16[512,1024]{1,0:T(8,128)(2,1)S(1)} %copy-done.1, f32[4,8,2,8,128]{4,3,2,1,0:T(8,128)S(1)} %copy-done.3, ...), custom_call_target="tpu_custom_call" | custom-call | tf_op jit(solution)/shard_map/pallas_call | solution.py:279
  73.7 137.5 %all-reduce.4.cloned.1.call-done = f32[32,8192]{1,0:T(8,128)} async-done(((f32[32,8192]{1,0:T(8,128)}), f32[32,8192]{1,0:T(8,128)}) %all-reduce.4.cloned.1.call-update) | async-done | bytes 1048592
  211.2 1.0 constant_dynamic-slice_fusion
  212.2 0.2 copy.29
  212.6 1.3 subtract_reduce_fusion.5
  213.9 1.3 add_reduce_fusion.4
  215.2 0.7 slice_add_fusion.3
  216.2 0.7 subtract_reduce_fusion
  217.0 2.7 %fusion.3 = f32[8,1024]{1,0:T(8,128)S(1)} fusion(f32[512,1024]{1,0:T(8,128)} %constant.43, f32[8,512]{1,0:T(8,128)S(1)} %stack.8, f32[8,512]{1,0:T(8,128)S(1)} %copy-done.9, f32[8,512]{1,0:T(8,128)S(1)} %stack.7, f32[8,512]{1,0:T(8,128)S(1)} %copy-done.8), kind=kOutput, calls=%fused_computation.43 | convolution fusion | flops 50343936 | bytes 2195456 | tf_op jit(solution)/shard_map/dot_general | solution.py:326
  219.7 1.1 fusion
  220.8 0.2 copy.30
  221.0 0.9 reshape.39
  (34 shorter events, 0.7 us)
Async XLA Ops:
  6.5 44.7 %copy-start = (bf16[512,1024]{1,0:T(8,128)(2,1)S(1)}, bf16[512,1024]{1,0:T(8,128)(2,1)}, u32[]{:S(2)}) copy-start(bf16[512,1024]{1,0:T(8,128)(2,1)} %constant.30.clone.high) | copy-start | bytes 3145732
  6.5 204.6 %all-reduce.4.cloned.1.call-start = ((), (), s32[]{:S(2)}) async-start(), calls=%async_computation | async-start | bytes 2097152
  51.3 1.2 copy-start.1
  52.5 1.2 copy-start.2
  53.8 0.9 copy-start.3
  54.7 0.9 copy-start.4
  55.6 156.8 %copy-start.7 = (f32[8,512]{0,1:T(8,128)S(1)}, f32[8,512]{0,1:T(8,128)}, u32[]{:S(2)}) copy-start(f32[8,512]{0,1:T(8,128)} %constant.33.clone) | copy-start | bytes 49156
  73.6 138.9 %copy-start.6 = (f32[1,8,512]{1,2,0:T(8,128)S(1)}, f32[1,8,512]{1,2,0:T(8,128)}, u32[]{:S(2)}) copy-start(f32[1,8,512]{1,2,0:T(8,128)} %constant.45) | copy-start | bytes 49156
  215.2 0.8 copy-start.10
  215.2 0.8 copy-start.11
  216.0 1.0 copy-start.8
  216.0 1.0 copy-start.9
  216.1 3.5 %copy-start.5 = (f32[512,1024]{1,0:T(8,128)S(1)}, f32[512,1024]{1,0:T(8,128)}, u32[]{:S(2)}) copy-start(f32[512,1024]{1,0:T(8,128)} %constant.44) | copy-start | bytes 6291460
Sparse Core Ops, SparseCore 0:
  73.8 137.3 all-reduce.3

commit v2 on v1

--- a/solution.py
+++ b/solution.py
@@ -186,7 +186,25 @@
     return [(r, i) for r in range(ROUNDS) for i in range(blocks) if i >= r + 1]
 
 
-def correlate_kernel(blocks, x, taps, pick, high, low, turns, onehot, out, xd, td, fx, fh, spec, cross):
+def rows_of_pairs(ids, owners, chan, hour):
+    depth = ids.shape[2]
+    nbins = owners.shape[1]
+    found = ids[0]
+    for i in range(1, ids.shape[0]):
+        found = found + ids[i]
+    bins = lax.broadcasted_iota(jnp.int32, (nbins, depth), 0) + 1
+    picked = (bins == found[0:1, :]).astype(jnp.float32).astype(jnp.bfloat16)
+    place = lax.broadcasted_iota(jnp.int32, (nbins, nbins), 0)
+    row = lax.rem(place, chan) * hour + lax.div(place, chan)
+    moved = (row == owners[...]).astype(jnp.float32).astype(jnp.bfloat16)
+    return jnp.dot(moved, picked, preferred_element_type=jnp.float32).astype(jnp.bfloat16)
+
+
+def correlate_kernel(
+    blocks, hour, x, taps, pick, high, low, turns, ids, owners, out, xd, td, fx, fh, spec, cross
+):
+    onehot = rows_of_pairs(ids, owners, blocks, hour)
+    cross[...] = jnp.zeros_like(cross)
     rows = x.shape[0]
     per = rows // blocks
     span = SPLIT * LANES
@@ -249,37 +267,45 @@
                 spec[k2, 0, here, :] = (xr * hr - xi * hi).astype(jnp.bfloat16).astype(jnp.float32)
                 spec[k2, 1, here, :] = (xr * hi + xi * hr).astype(jnp.bfloat16).astype(jnp.float32)
 
-        @pl.loop(0, SPLIT)
-        def _(k2):
-            for p, (r, i) in enumerate(pairs):
-                re = im = None
-                for c in range(per // 8):
-                    near = pl.ds(i * per + 8 * c, 8)
-                    far = pl.ds((i - r - 1) * per + 8 * c, 8)
-                    nr, ni = spec[k2, 0, near, :], spec[k2, 1, near, :]
-                    fr, fi = spec[k2, 0, far, :], spec[k2, 1, far, :]
-                    one, two = fr * nr + fi * ni, fi * nr - fr * ni
-                    re, im = (one, two) if re is None else (re + one, im + two)
-                cross[8 * p : 8 * p + 8, :LANES] = re
-                cross[8 * p : 8 * p + 8, LANES:] = im
-            total = cross[...]
-            top = total.astype(jnp.bfloat16)
-            rest = (total - top.astype(jnp.float32)).astype(jnp.bfloat16)
-            place = pl.multiple_of((t * SPLIT + k2) * 2 * LANES, 2 * LANES)
-            out[:, pl.ds(place, 2 * LANES)] = jnp.dot(
-                onehot[...], top, preferred_element_type=jnp.float32
-            ) + jnp.dot(onehot[...], rest, preferred_element_type=jnp.float32)
-
-
-def correlate(x, taps, onehot, blocks):
-    rows = x.shape[0]
+        @pl.loop(0, SPLIT // 2)
+        def _(kk):
+            both = []
+            for e in range(2):
+                k2 = 2 * kk + e
+                for r, i in pairs:
+                    p = i * ROUNDS + r
+                    re = im = None
+                    for c in range(per // 8):
+                        near = pl.ds(i * per + 8 * c, 8)
+                        far = pl.ds((i - r - 1) * per + 8 * c, 8)
+                        nr, ni = spec[k2, 0, near, :], spec[k2, 1, near, :]
+                        fr, fi = spec[k2, 0, far, :], spec[k2, 1, far, :]
+                        one, two = fr * nr + fi * ni, fi * nr - fr * ni
+                        re, im = (one, two) if re is None else (re + one, im + two)
+                    cross[8 * p : 8 * p + 8, :LANES] = re
+                    cross[8 * p : 8 * p + 8, LANES:] = im
+                total = cross[...]
+                top = total.astype(jnp.bfloat16)
+                rest = (total - top.astype(jnp.float32)).astype(jnp.bfloat16)
+                both.append(
+                    jnp.dot(onehot, top, preferred_element_type=jnp.float32)
+                    + jnp.dot(onehot, rest, preferred_element_type=jnp.float32)
+                )
+            for h in range(hour):
+                rows_of = slice(h * blocks, (h + 1) * blocks)
+                out[h, t * (SPLIT // 2) + kk] = jnp.concatenate(
+                    [both[0][rows_of], both[1][rows_of]], axis=0
+                ).astype(jnp.bfloat16)
+
+
+def correlate(x, taps, ids, owners, hour):
+    rows, blocks = x.shape[0], ids.shape[0]
     high, low = two_parts(sub_tables())
-    nbins, depth = onehot.shape
     vmem = pl.BlockSpec(memory_space=pltpu.VMEM)
     return pl.pallas_call(
-        functools.partial(correlate_kernel, blocks),
-        out_shape=jax.ShapeDtypeStruct((nbins, 2 * FR), jnp.float32),
-        in_specs=[vmem] * 7,
+        functools.partial(correlate_kernel, blocks, hour),
+        out_shape=jax.ShapeDtypeStruct((hour, TILES * SPLIT // 2, 2 * blocks, 2 * LANES), jnp.bfloat16),
+        in_specs=[vmem] * 8,
         out_specs=vmem,
         scratch_shapes=[
             pltpu.VMEM((SPLIT, rows, SUB), jnp.bfloat16),
@@ -287,48 +313,171 @@
             pltpu.VMEM((SPLIT, rows, 2 * SUB), jnp.float32),
             pltpu.VMEM((SPLIT, rows, 2 * SUB), jnp.float32),
             pltpu.VMEM((SPLIT, 2, rows, LANES), jnp.float32),
-            pltpu.VMEM((depth, 2 * LANES), jnp.float32),
+            pltpu.VMEM((ids.shape[2], 2 * LANES), jnp.float32),
         ],
         compiler_params=pltpu.CompilerParams(vmem_limit_bytes=48 * 2**20),
-    )(x, taps, jnp.asarray(pick_table()), jnp.asarray(high), jnp.asarray(low), jnp.asarray(turn_table()), onehot)
-
-
-def wave_of(row, norm):
-    tiles = row.reshape(TILES, SPLIT, 2, LANES).transpose(2, 1, 0, 3).reshape(2, SPLIT, SUB)
-    weight = np.full((SPLIT, SUB), 2.0)
-    weight[0, 0] = 1.0
-    tiles = tiles * jnp.asarray(weight.astype(np.float32) * np.float32(norm))
-    main = np.ones((SPLIT, SUB))
-    main[SPLIT // 2 :, 0] = 0.0
-    re, im = tiles[0] * main.astype(np.float32), tiles[1] * main.astype(np.float32)
-    got = small_dft([(re[k], im[k]) for k in range(SPLIT)], 1)
-    g_re = jnp.stack([v[0] for v in got])
-    g_im = jnp.stack([v[1] for v in got])
-    turn = 2.0 * np.pi * np.arange(SPLIT)[:, None] * np.arange(SUB)[None, :] / (2 * FR)
-    c, s = np.cos(turn).astype(np.float32), np.sin(turn).astype(np.float32)
-    y_re = g_re * c - g_im * s
-    y_im = g_re * s + g_im * c
+    )(
+        x,
+        taps,
+        jnp.asarray(pick_table()),
+        jnp.asarray(high),
+        jnp.asarray(low),
+        jnp.asarray(turn_table()),
+        ids,
+        owners.reshape(1, -1),
+    )
+
+
+def mix_table():
+    l2 = np.arange(SPLIT)[None, :]
+    k2 = np.arange(SPLIT)[:, None]
+    main = 2.0 * np.pi * k2 * l2 / SPLIT
+    extra = 2.0 * np.pi * ((k2 - SPLIT // 2) * l2 / SPLIT + l2 / (2 * SPLIT))
+    table = np.stack([np.cos(main), np.sin(main), np.cos(extra), np.sin(extra)])
+    return np.ascontiguousarray(np.broadcast_to(table[..., None], (4, SPLIT, SPLIT, LANES))).astype(np.float32)
+
+
+def back_table():
     l2 = np.arange(SPLIT)[:, None]
-    k2 = np.arange(SPLIT // 2)[None, :]
-    angle = 2.0 * np.pi * (k2 * l2 / SPLIT + l2 / (2 * SPLIT))
-    extra = jnp.sum(
-        np.cos(angle).astype(np.float32) * tiles[0, SPLIT // 2 :, 0][None, :]
-        - np.sin(angle).astype(np.float32) * tiles[1, SPLIT // 2 :, 0][None, :],
-        axis=1,
-    )
-    y_im = jnp.where(jnp.arange(SUB)[None, :] == 0, extra[:, None], y_im)
-    l1 = np.arange(2 * SUB)[None, :]
-    k1 = np.arange(SUB)[:, None]
-    turn = 2.0 * np.pi * ((k1 * l1) % (2 * SUB)) / (2 * SUB)
-    cos, sin = np.cos(turn), -np.sin(turn)
-    sin[0, :] = 1.0 - 2.0 * (np.arange(2 * SUB) % 2)
-    table = np.concatenate([cos, sin]).astype(np.float32)
-    wave = jnp.dot(jnp.concatenate([y_re, y_im], axis=1), jnp.asarray(table), precision=exact)
-    return wave.T.reshape(1, 2 * FR)
-
-
-def exchange_kernel(blocks, x, taps, ids, x_out, taps_out, ids_out, send, recv, keep):
+    turn = 2.0 * np.pi * l2 * np.arange(SUB)[None, :] / (2 * FR)
+    table = np.stack([np.cos(turn), np.sin(turn)]).reshape(2, SPLIT, TILES, LANES)
+    return np.ascontiguousarray(table.transpose(2, 0, 1, 3)).astype(np.float32)
+
+
+def over_lanes(a, b):
+    return lax.dot_general(a, b, (((1,), (1,)), ((), ())), preferred_element_type=jnp.float32)
+
+
+def inverse(row, mix, back, high, low, norm):
+    lane = lax.broadcasted_iota(jnp.int32, (SPLIT, LANES), 1)
+    slot = lax.broadcasted_iota(jnp.int32, (SPLIT, LANES), 0)
+    plain, flipped = [], []
+    for t in range(TILES):
+        re = row[t * SPLIT : (t + 1) * SPLIT, :LANES] * (2.0 * norm)
+        im = row[t * SPLIT : (t + 1) * SPLIT, LANES:] * (2.0 * norm)
+        main_re, main_im = re, im
+        if t == 0:
+            main_re = jnp.where(lane == 0, jnp.where(slot == 0, re * 0.5, re), re)
+            drop = (lane == 0) & (slot >= SPLIT // 2)
+            main_re = jnp.where(drop, 0.0, main_re)
+            main_im = jnp.where(drop, 0.0, im)
+        g_re = g_im = jnp.zeros((SPLIT, LANES), jnp.float32)
+        for k2 in range(SPLIT):
+            a, b = main_re[k2 : k2 + 1, :], main_im[k2 : k2 + 1, :]
+            c, s = mix[0, k2], mix[1, k2]
+            g_re = g_re + (c * a - s * b)
+            g_im = g_im + (s * a + c * b)
+        c, s = back[t, 0], back[t, 1]
+        y_re, y_im = g_re * c - g_im * s, g_re * s + g_im * c
+        if t == 0:
+            more = jnp.zeros((SPLIT, LANES), jnp.float32)
+            for k2 in range(SPLIT // 2, SPLIT):
+                more = more + (mix[2, k2] * re[k2 : k2 + 1, :] - mix[3, k2] * im[k2 : k2 + 1, :])
+            y_im = jnp.where(lane == 0, more, y_im)
+        sign = jnp.where(lax.rem(lane, 2) == 0, 1.0, -1.0)
+        plain += [y_re, y_im]
+        flipped += [y_re * sign, y_im * sign]
+    y = jnp.concatenate([jnp.concatenate(plain, axis=1), jnp.concatenate(flipped, axis=1)], axis=0)
+    top = y.astype(jnp.bfloat16)
+    rest = (y - top.astype(jnp.float32)).astype(jnp.bfloat16)
+    return over_lanes(top, high[...]) + (over_lanes(rest, high[...]) + over_lanes(top, low[...]))
+
+
+def reduce_kernel(
+    chan, hour, norm, part, high, low, mix, back, out, sums, first, second, send, recv, send2, recv2
+):
+    mine, my_hour = lax.axis_index("chan"), lax.axis_index("hour")
+    barrier = pltpu.get_barrier_semaphore()
+    for o in range(1, hour):
+        pl.semaphore_signal(
+            barrier, inc=1, device_id={"hour": lax.rem(my_hour + o, hour)}, device_id_type=MESH
+        )
+    for o in range(1, chan):
+        pl.semaphore_signal(
+            barrier, inc=1, device_id={"chan": lax.rem(mine + o, chan)}, device_id_type=MESH
+        )
+    pl.semaphore_wait(barrier, chan + hour - 2)
+    copies = []
+    for o in range(1, hour):
+        to = lax.rem(my_hour + o, hour)
+        copy = pltpu.make_async_remote_copy(
+            src_ref=part.at[to],
+            dst_ref=first.at[o],
+            send_sem=send.at[o],
+            recv_sem=recv.at[o],
+            device_id={"hour": to},
+            device_id_type=MESH,
+        )
+        copy.start()
+        copies.append(copy)
+    width = 2 * LANES
+    depth = chan * TILES * SPLIT
+    total = part[my_hour].astype(jnp.float32)
+    for o in range(1, hour):
+        copies[o - 1].wait_recv()
+        total = total + first[o].astype(jnp.float32)
+    total = total.reshape(depth, width).astype(jnp.bfloat16)
+    to_row = lax.broadcasted_iota(jnp.int32, (depth, depth), 0)
+    from_row = lax.broadcasted_iota(jnp.int32, (depth, depth), 1)
+    per = TILES * SPLIT
+    wanted = lax.rem(to_row, per) * chan + lax.div(to_row, per)
+    swap = (wanted == from_row).astype(jnp.float32).astype(jnp.bfloat16)
+    sums[...] = jnp.dot(swap, total, preferred_element_type=jnp.float32).astype(jnp.bfloat16).reshape(sums.shape)
+    later = []
+    for o in range(1, chan):
+        to = lax.rem(mine + o, chan)
+        copy = pltpu.make_async_remote_copy(
+            src_ref=sums.at[to],
+            dst_ref=second.at[o],
+            send_sem=send2.at[o],
+            recv_sem=recv2.at[o],
+            device_id={"chan": to},
+            device_id_type=MESH,
+        )
+        copy.start()
+        later.append(copy)
+    row = sums[mine].astype(jnp.float32)
+    for o in range(1, chan):
+        later[o - 1].wait_recv()
+        row = row + second[o].astype(jnp.float32)
+    out[...] = inverse(row, mix, back, high, low, norm)
+    for copy in copies + later:
+        copy.wait_send()
+
+
+def reduce(part, norm, chan, hour):
+    high, low = two_parts(sub_tables())
+    vmem = pl.BlockSpec(memory_space=pltpu.VMEM)
+    per = TILES * SPLIT
+    wave = pl.pallas_call(
+        functools.partial(reduce_kernel, chan, hour, norm),
+        out_shape=jax.ShapeDtypeStruct((2 * SPLIT, SUB), jnp.float32),
+        in_specs=[vmem] * 5,
+        out_specs=vmem,
+        scratch_shapes=[
+            pltpu.VMEM((chan, per, 2 * LANES), jnp.bfloat16),
+            pltpu.VMEM(part.shape, part.dtype),
+            pltpu.VMEM((chan, per, 2 * LANES), jnp.bfloat16),
+            pltpu.SemaphoreType.DMA((hour,)),
+            pltpu.SemaphoreType.DMA((hour,)),
+            pltpu.SemaphoreType.DMA((chan,)),
+            pltpu.SemaphoreType.DMA((chan,)),
+        ],
+        compiler_params=pltpu.CompilerParams(
+            collective_id=1, has_side_effects=True, vmem_limit_bytes=32 * 2**20
+        ),
+    )(part, jnp.asarray(high), jnp.asarray(low), jnp.asarray(mix_table()), jnp.asarray(back_table()))
+    return wave.reshape(2, SPLIT, SUB).transpose(0, 2, 1).reshape(1, 2 * FR)
+
+
+def exchange_kernel(blocks, x, taps, bin_ids, x_out, taps_out, ids_out, ids, send, recv, keep):
     me = lax.axis_index("chan")
+    place = lax.div(lax.broadcasted_iota(jnp.int32, ids.shape, 1), 8)
+    labels = jnp.zeros(ids.shape, jnp.int32)
+    for r in range(ROUNDS):
+        live = (place == me * ROUNDS + r) & (me >= r + 1)
+        labels = jnp.where(live, bin_ids[r : r + 1, :] + 1, labels)
+    ids[...] = labels
     barrier = pltpu.get_barrier_semaphore()
     for o in range(1, blocks):
         pl.semaphore_signal(
@@ -360,49 +509,37 @@
         copy.wait()
 
 
-def exchange(x, taps, ids, blocks):
+def exchange(x, taps, bin_ids, blocks):
     hbm = pl.BlockSpec(memory_space=pl.ANY)
     return pl.pallas_call(
         functools.partial(exchange_kernel, blocks),
         out_shape=(
             jax.ShapeDtypeStruct(x.shape, x.dtype),
             jax.ShapeDtypeStruct(taps.shape, taps.dtype),
-            jax.ShapeDtypeStruct((blocks,) + ids.shape, ids.dtype),
+            jax.ShapeDtypeStruct((blocks, 8, 8 * ROUNDS * blocks), jnp.int32),
         ),
-        in_specs=[hbm] * 3,
+        in_specs=[hbm, hbm, pl.BlockSpec(memory_space=pltpu.VMEM)],
         out_specs=(hbm,) * 3,
         scratch_shapes=[
+            pltpu.VMEM((8, 8 * ROUNDS * blocks), jnp.int32),
             pltpu.SemaphoreType.DMA((3, blocks)),
             pltpu.SemaphoreType.DMA((3, blocks)),
             pltpu.SemaphoreType.DMA((3,)),
         ],
         compiler_params=pltpu.CompilerParams(collective_id=0, has_side_effects=True),
-    )(x, taps, ids)
-
-
-def onehot_of(all_ids, owners, blocks):
-    pairs = pairs_of(blocks)
-    flat = jnp.stack([all_ids[r, i] for r, i in pairs])
-    nbins = owners.shape[0]
-    labels = jnp.arange(nbins, dtype=jnp.int32)
-    places = jnp.sum(jnp.where(flat[:, None] == labels[None, :], owners[None, :], 0), axis=1)
-    hot = (places[None, :] == labels[:, None]).astype(jnp.bfloat16)
-    return jnp.repeat(hot, 8, axis=1)
+    )(x, taps, bin_ids)
 
 
 def split_body(traces, taps, bin_ids, owners):
-    blocks = lax.axis_size("chan")
+    blocks, hour = lax.axis_size("chan"), lax.axis_size("hour")
     channels = traces.shape[0]
     per = channels // blocks
-    ids = jnp.broadcast_to(jnp.pad(bin_ids, ((0, 8 - ROUNDS), (0, 0))), (8, LANES))
-    x, filters, all_ids = exchange(
-        traces.reshape(blocks, per, FR), taps.reshape(blocks, per, taps.shape[1]), ids, blocks
+    x, filters, ids = exchange(
+        traces.reshape(blocks, per, FR), taps.reshape(blocks, per, taps.shape[1]), bin_ids, blocks
     )
-    onehot = onehot_of(all_ids[:, :ROUNDS, 0].T, owners, blocks)
-    stack = correlate(x.reshape(channels, FR), filters.reshape(channels, taps.shape[1]), onehot, blocks)
-    final = lax.psum_scatter(stack, ("chan", "hour"), scatter_dimension=0, tiled=True)
-    norm = 1.0 / (FR * math.sqrt(FR * lax.axis_size("hour") * channels))
-    return wave_of(final[0], norm)
+    part = correlate(x.reshape(channels, FR), filters.reshape(channels, taps.shape[1]), ids, owners, hour)
+    norm = 1.0 / (FR * math.sqrt(FR * hour * channels))
+    return reduce(part, norm, blocks, hour)
 
 
 def solution(mesh):
@@ -412,7 +549,8 @@
         chan, hour = mesh.shape["chan"], mesh.shape["hour"]
         channels = traces.shape[0] // chan
         fits = (
-            channels % (16 * chan) == 0
+            chan == 8
+            and channels % (16 * chan) == 0
             and traces.shape[1] == hour * FR
             and taps.shape[1] == SPLIT * LANES // 2
             and owners.shape[0] == chan * hour

time: 229 us -> 74.3 us (0.32)
  waiting for transfers between devices: 138 us -> 0 us
  Pallas kernels: 44.3 us -> 64 us
  local copies, waits for them, and re-layouts: 24.3 us -> 9.44 us
  between operations: 13.6 us -> 0.06 us
  other arithmetic: 5.21 us -> 0 us
  matrix products: 3.8 us -> 0 us
    unnamed x2 -> x0, waiting for transfers between devices: 138 us -> none
    pallas_call x1 -> x2, Pallas kernels: 18 us -> 36.6 us  [the longest x1 20.9 us: reduce(): pl.pallas_call(functools.partial(reduce_kernel, chan, hour, norm), out_sh...]
    another operation x3 -> x0, local copies, waits for them, and re-layouts: 13.9 us -> none  [the longest x1 13.8 us: onehot_of(): flat = jnp.stack([all_ids[r, i] for r, i in pairs])]
    dot_general x2 -> x0, matrix products: 3.8 us -> none  [wave_of(): jnp.dot(jnp.concatenate([y_re, y_im], axis=1), jnp.asarray(table), precis...]
    unnamed x25 -> x19, local copies, waits for them, and re-layouts: 5.32 us -> 8.33 us
  transfers between devices with their start and end apart: 1 -> 0, of which waited for: 1 -> 0; matrix products, arithmetic and copies ran while one was open for 0% -> 0% of each run, Pallas kernels for 0% -> 0%
where the time goes in v2:
time: 74.3 us; the launch traced here: 73.5 us
  Pallas kernels  64 us (86%)
  local copies, waits for them, and re-layouts  9.44 us (13%)
    pallas_call x1, Pallas kernels, exchange(): pl.pallas_call(functools.partial(exchange_kernel, blocks), out_shape=(jax...  27.4 us
    pallas_call x1, Pallas kernels, reduce(): pl.pallas_call(functools.partial(reduce_kernel, chan, hour, norm), out_sh...  20.9 us
    pallas_call x1, Pallas kernels, correlate(): pl.pallas_call(functools.partial(correlate_kernel, blocks, hour), out_sha...  15.7 us
    unnamed x19, local copies, waits for them, and re-layouts  8.33 us

profile of v2, /device:TPU:0, one launch (start us, length us, event | category | flops | bytes accessed | tf_op | source)
XLA Modules:
  0.0 73.5 jit_solution(2701284171545864452)
XLA Ops:
  0.0 1.3 %copy.15.bin_ids = s32[4,1]{1,0:T(4,128)} copy(s32[4,1]{0,1:T(1,128)} %param.14) | data formatting | bytes 32 | tf_op args[2]
  1.3 27.4 %shard_map.118 = (bf16[8,16,4096]{2,1,0:T(8,128)(2,1)}, bf16[8,16,512]{2,1,0:T(8,128)(2,1)}, s32[8,8,256]{2,1,0:T(8,128)}) custom-call(bf16[8,16,4096]{2,1,0:T(8,128)(2,1)} %bitcast.12, bf16[8,16,512]{2,1,0:T(8,128)(2,1)} %bitcast.13, s32[4,1]{1,0:T(4,128)} %copy.15.bin_ids), custom_call_target="tpu_custom_call" | custom-call | tf_op jit(solution)/shard_map/pallas_call | solution.py:514
  28.7 0.0 copy-start
  28.7 1.2 %copy-done = bf16[512,1024]{1,0:T(8,128)(2,1)S(1)} copy-done((bf16[512,1024]{1,0:T(8,128)(2,1)S(1)}, bf16[512,1024]{1,0:T(8,128)(2,1)}, u32[]{:S(2)}) %copy-start) | copy-done | bytes 1048600
  29.9 0.0 copy-start.1
  29.9 1.2 %copy-done.1 = bf16[512,1024]{1,0:T(8,128)(2,1)S(1)} copy-done((bf16[512,1024]{1,0:T(8,128)(2,1)S(1)}, bf16[512,1024]{1,0:T(8,128)(2,1)}, u32[]{:S(2)}) %copy-start.1) | copy-done | bytes 1048600
  31.2 0.0 copy-start.2
  31.2 1.2 %copy-done.2 = bf16[8,16,4096]{2,1,0:T(8,128)(2,1)S(1)} copy-done((bf16[8,16,4096]{2,1,0:T(8,128)(2,1)S(1)}, bf16[8,16,4096]{2,1,0:T(8,128)(2,1)}, u32[]{:S(2)}) %copy-start.2) | copy-done | bytes 1048600
  32.4 0.0 copy-start.3
  32.4 0.9 %copy-done.3 = f32[4,8,2,8,128]{4,3,2,1,0:T(8,128)S(1)} copy-done((f32[4,8,2,8,128]{4,3,2,1,0:T(8,128)S(1)}, f32[4,8,2,8,128]{4,3,2,1,0:T(8,128)}, u32[]{:S(2)}) %copy-start.3) | copy-done | bytes 262168
  33.3 0.0 copy-start.5
  33.3 0.9 %copy-done.5 = bf16[8,16,512]{2,1,0:T(8,128)(2,1)S(1)} copy-done((bf16[8,16,512]{2,1,0:T(8,128)(2,1)S(1)}, bf16[8,16,512]{2,1,0:T(8,128)(2,1)}, u32[]{:S(2)}) %copy-start.5) | copy-done | bytes 131096
  34.2 0.0 copy-start.6
  34.2 0.8 %copy-done.6 = s32[8,8,256]{2,1,0:T(8,128)S(1)} copy-done((s32[8,8,256]{2,1,0:T(8,128)S(1)}, s32[8,8,256]{2,1,0:T(8,128)}, u32[]{:S(2)}) %copy-start.6) | copy-done | bytes 65560
  35.1 0.0 copy-start.8
  35.1 0.7 copy-done.8
  35.7 0.0 copy-start.4
  35.7 0.0 copy-start.7
  35.7 15.7 %shard_map.119.part = bf16[4,16,16,256]{3,2,1,0:T(8,128)(2,1)S(1)} custom-call(bf16[128,4096]{1,0:T(8,128)(2,1)S(1)} %bitcast.7, bf16[128,512]{1,0:T(8,128)(2,1)S(1)} %bitcast.9, bf16[1024,1024]{1,0:T(8,128)(2,1)} %constant.12.clone.pick, bf16[512,1024]{1,0:T(8,128)(2,1)S(1)} %copy-done.1, bf16[512,1024]{1,0:T(8,128)(2,1)S(1)} %copy-done, ...), custom_call_target="tpu_custom_call" | custom-call | tf_op jit(solution)/shard_map/pallas_call | solution.py:305
  51.5 0.0 copy-done.4
  51.5 0.0 copy-done.7
  51.5 20.9 %shard_map.120 = f32[16,512]{1,0:T(8,128)S(1)} custom-call(bf16[4,16,16,256]{3,2,1,0:T(8,128)(2,1)S(1)} %shard_map.119.part, bf16[512,1024]{1,0:T(8,128)(2,1)S(1)} %copy-done.1, bf16[512,1024]{1,0:T(8,128)(2,1)S(1)} %copy-done, f32[4,8,8,128]{3,2,1,0:T(8,128)S(1)} %copy-done.4, f32[4,2,8,128]{3,2,1,0:T(8,128)S(1)} %copy-done.7), custom_call_target="tpu_custom_call" | custom-call | tf_op jit(solution)/shard_map/pallas_call | solution.py:452
  72.4 0.2 copy.16
  72.6 0.9 %reshape.27 = f32[1,8192]{1,0:T(1,128)} reshape(f32[2,512,8]{2,1,0:T(8,128)S(1)} %bitcast.11) | data formatting | bytes 65536 | tf_op jit(solution)/shard_map/reshape | solution.py:470
Async XLA Ops:
  28.7 1.2 %copy-start = (bf16[512,1024]{1,0:T(8,128)(2,1)S(1)}, bf16[512,1024]{1,0:T(8,128)(2,1)}, u32[]{:S(2)}) copy-start(bf16[512,1024]{1,0:T(8,128)(2,1)} %constant.14.clone.low) | copy-start | bytes 3145732
  29.9 1.2 %copy-start.1 = (bf16[512,1024]{1,0:T(8,128)(2,1)S(1)}, bf16[512,1024]{1,0:T(8,128)(2,1)}, u32[]{:S(2)}) copy-start(bf16[512,1024]{1,0:T(8,128)(2,1)} %constant.13.clone.high) | copy-start | bytes 3145732
  31.2 1.2 %copy-start.2 = (bf16[8,16,4096]{2,1,0:T(8,128)(2,1)S(1)}, bf16[8,16,4096]{2,1,0:T(8,128)(2,1)}, u32[]{:S(2)}) copy-start(bf16[8,16,4096]{2,1,0:T(8,128)(2,1)} %get-tuple-element.8) | copy-start | bytes 3145732
  32.4 0.9 %copy-start.3 = (f32[4,8,2,8,128]{4,3,2,1,0:T(8,128)S(1)}, f32[4,8,2,8,128]{4,3,2,1,0:T(8,128)}, u32[]{:S(2)}) copy-start(f32[4,8,2,8,128]{4,3,2,1,0:T(8,128)} %constant.15.clone.turns) | copy-start | bytes 786436
  33.3 0.9 %copy-start.5 = (bf16[8,16,512]{2,1,0:T(8,128)(2,1)S(1)}, bf16[8,16,512]{2,1,0:T(8,128)(2,1)}, u32[]{:S(2)}) copy-start(bf16[8,16,512]{2,1,0:T(8,128)(2,1)} %get-tuple-element.9) | copy-start | bytes 393220
  34.2 0.8 %copy-start.6 = (s32[8,8,256]{2,1,0:T(8,128)S(1)}, s32[8,8,256]{2,1,0:T(8,128)}, u32[]{:S(2)}) copy-start(s32[8,8,256]{2,1,0:T(8,128)} %get-tuple-element.10.ids) | copy-start | bytes 196612
  35.1 0.7 copy-start.8
  35.7 15.7 %copy-start.4 = (f32[4,8,8,128]{3,2,1,0:T(8,128)S(1)}, f32[4,8,8,128]{3,2,1,0:T(8,128)}, u32[]{:S(2)}) copy-start(f32[4,8,8,128]{3,2,1,0:T(8,128)} %constant.16.clone.mix) | copy-start | bytes 393220
  35.7 15.7 %copy-start.7 = (f32[4,2,8,128]{3,2,1,0:T(8,128)S(1)}, f32[4,2,8,128]{3,2,1,0:T(8,128)}, u32[]{:S(2)}) copy-start(f32[4,2,8,128]{3,2,1,0:T(8,128)} %constant.17.clone.back) | copy-start | bytes 98308

commit v3 on v0

--- a/solution.py
+++ b/solution.py
@@ -1,16 +1,20 @@
+import functools
 import math
 
 import jax
 import jax.numpy as jnp
+import numpy as np
 from jax import lax
+from jax.experimental import pallas as pl
+from jax.experimental.pallas import tpu as pltpu
 from jax.sharding import PartitionSpec as P
 
 FR = 4096
 ROUNDS = 4
+MESH = pl.DeviceIdType.MESH
 
 
 exact = lax.Precision.HIGHEST
-
 
 def passed_along(shard, axis, by):
     devices = lax.axis_size(axis)
@@ -107,9 +111,461 @@
     norm = 1.0 / (FR * math.sqrt(FR * lax.axis_size("hour") * frames * channels))
     return wave_re * norm
 
+SPLIT = 8
+SUB = FR // SPLIT
+LANES = 128
+TILES = SUB // LANES
+
+
+def sub_tables():
+    a = np.arange(SUB)[:, None]
+    k1 = np.arange(SUB)[None, :]
+    turn = 2.0 * np.pi * ((a * k1) % (2 * SUB)) / (2 * SUB)
+    cos, sin = np.cos(turn), -np.sin(turn)
+    sin[:, 0] = 1.0 - 2.0 * (np.arange(SUB) % 2)
+    table = np.stack([cos.reshape(SUB, TILES, LANES), sin.reshape(SUB, TILES, LANES)], axis=2)
+    return table.reshape(SUB, 2 * SUB)
+
+
+def two_parts(table):
+    high = table.astype(jnp.bfloat16)
+    low = (table - high.astype(np.float64)).astype(jnp.bfloat16)
+    return high, low
+
+
+def pick_table():
+    span = SPLIT * LANES
+    table = np.zeros((span, span), np.float32)
+    for n in range(SPLIT):
+        for b in range(LANES):
+            table[SPLIT * b + n, n * LANES + b] = 1.0
+    return table.astype(jnp.bfloat16)
+
+
+def turn_table():
+    n = np.arange(SPLIT)[:, None]
+    k1 = np.arange(SUB)[None, :]
+    turn = 2.0 * np.pi * n * k1 / (2 * FR)
+    table = np.stack([np.cos(turn), -np.sin(turn)], axis=1).reshape(SPLIT, 2, TILES, 1, LANES)
+    table = np.broadcast_to(table.transpose(2, 0, 1, 3, 4), (TILES, SPLIT, 2, 8, LANES))
+    return np.ascontiguousarray(table).astype(np.float32)
+
+
+def times(value, angle):
+    re, im = value
+    c, s = math.cos(angle), math.sin(angle)
+    if abs(s) < 1e-12:
+        return (re, im) if c > 0 else (-re, -im)
+    if abs(c) < 1e-12:
+        return (-im, re) if s > 0 else (im, -re)
+    if abs(abs(c) - abs(s)) < 1e-12:
+        root = abs(c)
+        p, q = math.copysign(1.0, c), math.copysign(1.0, s)
+        first = (re if p > 0 else -re) + (-im if q > 0 else im)
+        second = (re if q > 0 else -re) + (im if p > 0 else -im)
+        return first * root, second * root
+    return re * c - im * s, re * s + im * c
+
+
+def small_dft(values, sign, half=False):
+    size = len(values)
+    if size == 1:
+        return values
+    even = small_dft(values[0::2], sign)
+    odd = small_dft(values[1::2], sign)
+    low, high = [], []
+    for k in range(size // 2):
+        turned = times(odd[k], sign * 2.0 * math.pi * k / size)
+        low.append((even[k][0] + turned[0], even[k][1] + turned[1]))
+        if not half:
+            high.append((even[k][0] - turned[0], even[k][1] - turned[1]))
+    return low + high
+
+
+def pairs_of(blocks):
+    return [(r, i) for r in range(ROUNDS) for i in range(blocks) if i >= r + 1]
+
+
+def rows_of_pairs(ids, owners, chan, hour):
+    depth = ids.shape[1]
+    nbins = owners.shape[1]
+    bins = lax.broadcasted_iota(jnp.int32, (nbins, depth), 0) + 1
+    picked = (bins == ids[0:1, :]).astype(jnp.float32).astype(jnp.bfloat16)
+    place = lax.broadcasted_iota(jnp.int32, (nbins, nbins), 0)
+    row = lax.rem(place, chan) * hour + lax.div(place, chan)
+    moved = (row == owners[...]).astype(jnp.float32).astype(jnp.bfloat16)
+    return jnp.dot(moved, picked, preferred_element_type=jnp.float32).astype(jnp.bfloat16)
+
+
+def mix_table():
+    l2 = np.arange(SPLIT)[None, :]
+    k2 = np.arange(SPLIT)[:, None]
+    main = 2.0 * np.pi * k2 * l2 / SPLIT
+    extra = 2.0 * np.pi * ((k2 - SPLIT // 2) * l2 / SPLIT + l2 / (2 * SPLIT))
+    table = np.stack([np.cos(main), np.sin(main), np.cos(extra), np.sin(extra)])
+    return np.ascontiguousarray(np.broadcast_to(table[..., None], (4, SPLIT, SPLIT, LANES))).astype(np.float32)
+
+
+def back_table():
+    l2 = np.arange(SPLIT)[:, None]
+    turn = 2.0 * np.pi * l2 * np.arange(SUB)[None, :] / (2 * FR)
+    table = np.stack([np.cos(turn), np.sin(turn)]).reshape(2, SPLIT, TILES, LANES)
+    return np.ascontiguousarray(table.transpose(2, 0, 1, 3)).astype(np.float32)
+
+
+def over_lanes(a, b):
+    return lax.dot_general(a, b, (((1,), (1,)), ((), ())), preferred_element_type=jnp.float32)
+
+
+def inverse(row, mix, back, high, low, norm):
+    lane = lax.broadcasted_iota(jnp.int32, (SPLIT, LANES), 1)
+    slot = lax.broadcasted_iota(jnp.int32, (SPLIT, LANES), 0)
+    plain, flipped = [], []
+    for t in range(TILES):
+        re = row[t * SPLIT : (t + 1) * SPLIT, :LANES] * (2.0 * norm)
+        im = row[t * SPLIT : (t + 1) * SPLIT, LANES:] * (2.0 * norm)
+        main_re, main_im = re, im
+        if t == 0:
+            main_re = jnp.where(lane == 0, jnp.where(slot == 0, re * 0.5, re), re)
+            drop = (lane == 0) & (slot >= SPLIT // 2)
+            main_re = jnp.where(drop, 0.0, main_re)
+            main_im = jnp.where(drop, 0.0, im)
+        g_re = g_im = jnp.zeros((SPLIT, LANES), jnp.float32)
+        for k2 in range(SPLIT):
+            a, b = main_re[k2 : k2 + 1, :], main_im[k2 : k2 + 1, :]
+            c, s = mix[0, k2], mix[1, k2]
+            g_re = g_re + (c * a - s * b)
+            g_im = g_im + (s * a + c * b)
+        c, s = back[t, 0], back[t, 1]
+        y_re, y_im = g_re * c - g_im * s, g_re * s + g_im * c
+        if t == 0:
+            more = jnp.zeros((SPLIT, LANES), jnp.float32)
+            for k2 in range(SPLIT // 2, SPLIT):
+                more = more + (mix[2, k2] * re[k2 : k2 + 1, :] - mix[3, k2] * im[k2 : k2 + 1, :])
+            y_im = jnp.where(lane == 0, more, y_im)
+        sign = jnp.where(lax.rem(lane, 2) == 0, 1.0, -1.0)
+        plain += [y_re, y_im]
+        flipped += [y_re * sign, y_im * sign]
+    y = jnp.concatenate([jnp.concatenate(plain, axis=1), jnp.concatenate(flipped, axis=1)], axis=0)
+    top = y.astype(jnp.bfloat16)
+    rest = (y - top.astype(jnp.float32)).astype(jnp.bfloat16)
+    return over_lanes(top, high[...]) + (over_lanes(rest, high[...]) + over_lanes(top, low[...]))
+
+
+def kernel(chan, hour, norm, x, taps, bin_ids, owners, *refs):
+    tables, out = refs[:6], refs[6]
+    held = refs[7:13]
+    pick, high, low, turns, mix, back = held
+    xin, tin, ids, ids_in, xd, td, fx, fh, spec, cross, part, first, sums, second = refs[13:27]
+    table_sem, own_sem, ids_send, ids_recv, t_send, t_recv, x_send, x_recv = refs[27:35]
+    f_send, f_recv, send, recv, send2, recv2 = refs[35:]
+    me, my_hour = lax.axis_index("chan"), lax.axis_index("hour")
+    per = xin.shape[1]
+    span = SPLIT * LANES
+    share = pl.ds(pl.multiple_of(my_hour * (tin.shape[2] // hour), LANES), tin.shape[2] // hour)
+
+    def partner(o):
+        to, bit = me, 1
+        while bit < chan:
+            to = to + lax.rem(lax.div(o, bit), 2) * bit * (1 - 2 * lax.rem(lax.div(me, bit), 2))
+            bit *= 2
+        return to
+
+    def sent(src, dst, sends, recvs, **device):
+        return pltpu.make_async_remote_copy(
+            src_ref=src, dst_ref=dst, send_sem=sends, recv_sem=recvs, device_id=device, device_id_type=MESH
+        )
+
+    loads = [pltpu.make_async_copy(src, dst, table_sem.at[z]) for z, (src, dst) in enumerate(zip(tables, held))]
+    own = [
+        pltpu.make_async_copy(x.at[me], xin.at[me], own_sem.at[0]),
+        pltpu.make_async_copy(taps.at[me, :, share], tin.at[me, :, share], own_sem.at[1]),
+    ]
+    for copy in own + loads:
+        copy.start()
+    barrier = pltpu.get_barrier_semaphore()
+    for o in range(1, hour):
+        pl.semaphore_signal(
+            barrier, inc=1, device_id={"hour": lax.rem(my_hour + o, hour)}, device_id_type=MESH
+        )
+    for o in range(1, chan):
+        pl.semaphore_signal(barrier, inc=1, device_id={"chan": partner(o)}, device_id_type=MESH)
+    place = lax.div(lax.broadcasted_iota(jnp.int32, ids.shape, 1), 8)
+    labels = jnp.zeros(ids.shape, jnp.int32)
+    for r in range(ROUNDS):
+        live = (place == me * ROUNDS + r) & (me >= r + 1)
+        labels = jnp.where(live, bin_ids[:, r : r + 1] + 1, labels)
+    ids[...] = labels
+    pl.semaphore_wait(barrier, chan + hour - 2)
+
+    def x_copy(o):
+        to = partner(o)
+        return sent(x.at[to], xin.at[me], x_send.at[o], x_recv.at[o], chan=to)
+
+    far_first = sorted(range(1, chan), key=lambda o: -(o.bit_length()))
+    tap_copies, id_copies = [], []
+    for o in far_first:
+        to = partner(o)
+        tap_copies.append(
+            sent(taps.at[to, :, share], tin.at[me, :, share], t_send.at[o], t_recv.at[o], chan=to)
+        )
+        tap_copies[-1].start()
+        x_copy(o).start()
+    for o in far_first:
+        id_copies.append(sent(ids, ids_in.at[o], ids_send.at[o], ids_recv.at[o], chan=partner(o)))
+        id_copies[-1].start()
+    for copy in own + loads:
+        copy.wait()
+
+    def take(block):
+        rows = pl.ds(pl.multiple_of(block * per, per), per)
+        flat = jnp.concatenate([xin[block, :, q * span : (q + 1) * span] for q in range(FR // span)], axis=0)
+        got = jnp.dot(flat, pick[...], preferred_element_type=jnp.float32).astype(jnp.bfloat16)
+        for q in range(FR // span):
+            for n in range(SPLIT):
+                xd[n * per : (n + 1) * per, q * LANES : (q + 1) * LANES] = got[
+                    q * per : (q + 1) * per, n * LANES : (n + 1) * LANES
+                ]
+        found = jnp.dot(xd[...], high[...], preferred_element_type=jnp.float32) + jnp.dot(
+            xd[...], low[...], preferred_element_type=jnp.float32
+        )
+        for n in range(SPLIT):
+            fx[n, rows, :] = found[n * per : (n + 1) * per]
+
+    take(me)
+    for copy in tap_copies:
+        copy.wait_recv()
+    forwards = []
+    for o in range(1, hour):
+        to = lax.rem(my_hour + o, hour)
+        forwards.append(sent(tin.at[:, :, share], tin.at[:, :, share], f_send.at[o], f_recv.at[o], hour=to))
+        forwards[-1].start()
+
+    @pl.loop(1, chan // 2)
+    def _(o):
+        x_copy(o).wait_recv()
+        take(partner(o))
+
+    for copy in forwards:
+        copy.wait_recv()
+    count = tin.shape[2]
+    got = jnp.dot(
+        tin[...].reshape(chan * per, count), pick[:count, :], preferred_element_type=jnp.float32
+    ).astype(jnp.bfloat16)
+    for n in range(SPLIT):
+        td[n] = got[:, n * LANES : (n + 1) * LANES]
+
+    @pl.loop(0, SPLIT)
+    def _(n):
+        fh[n] = jnp.dot(td[n], high[:LANES, :], preferred_element_type=jnp.float32) + jnp.dot(
+            td[n], low[:LANES, :], preferred_element_type=jnp.float32
+        )
+
+    for copy in id_copies:
+        copy.wait_recv()
+    labels = ids[...]
+    for o in range(1, chan):
+        labels = labels + ids_in[o]
+    onehot = rows_of_pairs(labels, owners, chan, hour)
+    cross[...] = jnp.zeros_like(cross)
+
+    @pl.loop(chan // 2, chan)
+    def _(o):
+        x_copy(o).wait_recv()
+        take(partner(o))
+
+    pairs = pairs_of(chan)
+    lane0 = lax.broadcasted_iota(jnp.int32, (8, LANES), 1) == 0
+    steps = SPLIT // 2
+
+    def part_copy(t, o):
+        to = lax.rem(my_hour + o, hour)
+        where = pl.ds(t * steps, steps)
+        return sent(part.at[to, where], first.at[o, where], send.at[t, o], recv.at[t, o], hour=to)
+
+    def tile(t, edge):
+        @pl.loop(0, chan * per // 8)
+        def _(g):
+            here = pl.ds(pl.multiple_of(8 * g, 8), 8)
+
+            def bins_of(f):
+                values, extra = [], []
+                for n in range(SPLIT):
+                    re = f[n, here, pl.ds(pl.multiple_of(2 * t * LANES, LANES), LANES)]
+                    im = f[n, here, pl.ds(pl.multiple_of((2 * t + 1) * LANES, LANES), LANES)]
+                    if edge:
+                        angle = -math.pi * n / SPLIT
+                        extra.append((im * math.cos(angle), im * math.sin(angle)))
+                        im = jnp.where(lane0, 0.0, im)
+                    if n == 0:
+                        values.append((re, im))
+                    else:
+                        c, s = turns[t, n, 0], turns[t, n, 1]
+                        values.append((re * c - im * s, re * s + im * c))
+                found = small_dft(values, -1)
+                if edge:
+                    more = small_dft(extra, -1, half=True)
+                    for k2 in range(SPLIT // 2):
+                        old = found[SPLIT // 2 + k2]
+                        found[SPLIT // 2 + k2] = tuple(
+                            jnp.where(lane0, more[k2][z], old[z]) for z in range(2)
+                        )
+                return found
+
+            freq = bins_of(fx)
+            resp = bins_of(fh)
+            for k2 in range(SPLIT):
+                (xr, xi), (hr, hi) = freq[k2], resp[k2]
+                spec[k2, 0, here, :] = (xr * hr - xi * hi).astype(jnp.bfloat16).astype(jnp.float32)
+                spec[k2, 1, here, :] = (xr * hi + xi * hr).astype(jnp.bfloat16).astype(jnp.float32)
+
+        @pl.loop(0, steps)
+        def _(kk):
+            both = []
+            for e in range(2):
+                k2 = 2 * kk + e
+                for r, i in pairs:
+                    p = i * ROUNDS + r
+                    re = im = None
+                    for c in range(per // 8):
+                        near = pl.ds(i * per + 8 * c, 8)
+                        far = pl.ds((i - r - 1) * per + 8 * c, 8)
+                        nr, ni = spec[k2, 0, near, :], spec[k2, 1, near, :]
+                        fr, fi = spec[k2, 0, far, :], spec[k2, 1, far, :]
+                        one, two = fr * nr + fi * ni, fi * nr - fr * ni
+                        re, im = (one, two) if re is None else (re + one, im + two)
+                    cross[8 * p : 8 * p + 8, :LANES] = re
+                    cross[8 * p : 8 * p + 8, LANES:] = im
+                total = cross[...]
+                top = total.astype(jnp.bfloat16)
+                rest = (total - top.astype(jnp.float32)).astype(jnp.bfloat16)
+                both.append(
+                    jnp.dot(onehot, top, preferred_element_type=jnp.float32)
+                    + jnp.dot(onehot, rest, preferred_element_type=jnp.float32)
+                )
+            for h in range(hour):
+                rows_of = slice(h * chan, (h + 1) * chan)
+                part[h, t * steps + kk] = jnp.concatenate(
+                    [both[0][rows_of], both[1][rows_of]], axis=0
+                ).astype(jnp.bfloat16)
+
+        for o in range(1, hour):
+            part_copy(t, o).start()
+
+    tile(0, True)
+
+    @pl.loop(1, TILES)
+    def _(t):
+        tile(t, False)
+
+    width = 2 * LANES
+    depth = chan * TILES * SPLIT
+    for t in range(TILES):
+        for o in range(1, hour):
+            part_copy(t, o).wait_recv()
+    total = part[my_hour].astype(jnp.float32)
+    for o in range(1, hour):
+        total = total + first[o].astype(jnp.float32)
+    total = total.reshape(depth, width).astype(jnp.bfloat16)
+    to_row = lax.broadcasted_iota(jnp.int32, (depth, depth), 0)
+    from_row = lax.broadcasted_iota(jnp.int32, (depth, depth), 1)
+    slots = TILES * SPLIT
+    wanted = lax.rem(to_row, slots) * chan + lax.div(to_row, slots)
+    swap = (wanted == from_row).astype(jnp.float32).astype(jnp.bfloat16)
+    sums[...] = jnp.dot(swap, total, preferred_element_type=jnp.float32).astype(jnp.bfloat16).reshape(sums.shape)
+    later = []
+    for o in far_first:
+        to = partner(o)
+        later.append(sent(sums.at[to], second.at[o], send2.at[o], recv2.at[o], chan=to))
+        later[-1].start()
+    row = sums[me].astype(jnp.float32)
+    for copy in later:
+        copy.wait_recv()
+    for o in range(1, chan):
+        row = row + second[o].astype(jnp.float32)
+    out[...] = inverse(row, mix, back, high, low, norm)
+    for copy in tap_copies + id_copies + forwards + later:
+        copy.wait_send()
+    for o in range(1, chan):
+        x_copy(o).wait_send()
+    for t in range(TILES):
+        for o in range(1, hour):
+            part_copy(t, o).wait_send()
+
+
+def split_body(traces, taps, bin_ids, owners):
+    chan, hour = lax.axis_size("chan"), lax.axis_size("hour")
+    channels, count = taps.shape
+    per = channels // chan
+    norm = 1.0 / (FR * math.sqrt(FR * hour * channels))
+    high, low = two_parts(sub_tables())
+    tables = [pick_table(), high, low, turn_table(), mix_table(), back_table()]
+    depth = 8 * ROUNDS * chan
+    slots = TILES * SPLIT
+    part = (hour, slots // 2, 2 * chan, 2 * LANES)
+    sums = (chan, slots, 2 * LANES)
+    vmem, hbm = pl.BlockSpec(memory_space=pltpu.VMEM), pl.BlockSpec(memory_space=pl.ANY)
+    sems = pltpu.SemaphoreType.DMA
+    wave = pl.pallas_call(
+        functools.partial(kernel, chan, hour, norm),
+        out_shape=jax.ShapeDtypeStruct((2 * SPLIT, SUB), jnp.float32),
+        in_specs=[hbm, hbm, vmem, vmem] + [hbm] * len(tables),
+        out_specs=vmem,
+        scratch_shapes=[pltpu.VMEM(table.shape, table.dtype) for table in tables]
+        + [
+            pltpu.VMEM((chan, per, FR), jnp.bfloat16),
+            pltpu.VMEM((chan, per, count), jnp.bfloat16),
+            pltpu.VMEM((8, depth), jnp.int32),
+            pltpu.VMEM((chan, 8, depth), jnp.int32),
+            pltpu.VMEM((SPLIT * per, SUB), jnp.bfloat16),
+            pltpu.VMEM((SPLIT, channels, LANES), jnp.bfloat16),
+            pltpu.VMEM((SPLIT, channels, 2 * SUB), jnp.float32),
+            pltpu.VMEM((SPLIT, channels, 2 * SUB), jnp.float32),
+            pltpu.VMEM((SPLIT, 2, channels, LANES), jnp.float32),
+            pltpu.VMEM((depth, 2 * LANES), jnp.float32),
+            pltpu.VMEM(part, jnp.bfloat16),
+            pltpu.VMEM(part, jnp.bfloat16),
+            pltpu.VMEM(sums, jnp.bfloat16),
+            pltpu.VMEM(sums, jnp.bfloat16),
+            sems((len(tables),)),
+            sems((2,)),
+        ]
+        + [sems((chan,))] * 6
+        + [sems((hour,))] * 2
+        + [sems((TILES, hour))] * 2
+        + [sems((chan,))] * 2,
+        compiler_params=pltpu.CompilerParams(
+            collective_id=0, has_side_effects=True, vmem_limit_bytes=56 * 2**20
+        ),
+    )(
+        traces.reshape(chan, per, FR),
+        taps.reshape(chan, per, count),
+        bin_ids.T,
+        owners.reshape(1, -1),
+        *[jnp.asarray(table) for table in tables],
+    )
+    return wave.reshape(2, SPLIT, SUB).transpose(0, 2, 1).reshape(1, 2 * FR)
+
 
 def solution(mesh):
     placed = (P("chan", "hour"), P("chan", None), P(None, "chan"), P())
-    return jax.shard_map(
-        body, mesh=mesh, in_specs=placed, out_specs=P(("chan", "hour"), None), check_vma=False
-    )
+
+    def whole(traces, taps, bin_ids, owners):
+        chan, hour = mesh.shape["chan"], mesh.shape["hour"]
+        channels = traces.shape[0] // chan
+        fits = (
+            chan == 8
+            and channels % (16 * chan) == 0
+            and traces.shape[1] == hour * FR
+            and taps.shape[1] == SPLIT * LANES // 2
+            and owners.shape[0] == chan * hour
+        )
+        return jax.shard_map(
+            split_body if fits else body,
+            mesh=mesh,
+            in_specs=placed,
+            out_specs=P(("chan", "hour"), None),
+            check_vma=False,
+        )(traces, taps, bin_ids, owners)
+
+    return whole

time: 511 us -> 60.1 us (0.12)
  waiting for transfers between devices: 289 us -> 0 us
  starting transfers between devices: 94.5 us -> 0 us
  matrix products: 62.2 us -> 0 us
  Pallas kernels: 0 us -> 58.1 us
  local copies, waits for them, and re-layouts: 37.8 us -> 1.86 us
  between operations: 14.3 us -> 0.02 us
  other arithmetic: 12.1 us -> 0 us
    unnamed x4 -> x0, waiting for transfers between devices: 244 us -> none
    ppermute x8 -> x0, starting transfers between devices: 94.5 us -> none  [passed_along(): return lax.ppermute(shard, axis, pairs)]
    dot_general x19 -> x0, matrix products: 62.2 us -> none  [the longest x3 14.7 us: transform(): section_im = jnp.einsum('...an,ak->...nk', grid, sin_one, precision=exact)]
    pallas_call x0 -> x1, Pallas kernels: none -> 58.1 us  [split_body(): pl.pallas_call(functools.partial(kernel, chan, hour, norm), out_shape=jax...]
    ppermute x8 -> x0, waiting for transfers between devices: 45.3 us -> none  [passed_along(): return lax.ppermute(shard, axis, pairs)]
    add x2 -> x0, local copies, waits for them, and re-layouts: 10.8 us -> none  [transform(): turned_im = section_re * sin_turn + section_im * cos_turn]
    sub x2 -> x0, local copies, waits for them, and re-layouts: 10.8 us -> none  [transform(): turned_re = section_re * cos_turn - section_im * sin_turn]
    reduce_sum x2 -> x0, other arithmetic: 5.52 us -> none  [the longest x1 5.34 us: body(): cross_re = jnp.sum(far_re * near_re + far_im * near_im, axis=(0, 1))]
  transfers between devices with their start and end apart: 10 -> 0, of which waited for: 5 -> 0; matrix products, arithmetic and copies ran while one was open for 0% -> 0% of each run, Pallas kernels for 0% -> 0%
where the time goes in v3:
time: 60.1 us; the launch traced here: 59.9 us
  Pallas kernels  58.1 us (97%)
  local copies, waits for them, and re-layouts  1.86 us (3%)
    pallas_call x1, Pallas kernels, split_body(): pl.pallas_call(functools.partial(kernel, chan, hour, norm), out_shape=jax...  58.1 us
    reshape x2, local copies, waits for them, and re-layouts, split_body(): return wave.reshape(2, SPLIT, SUB).transpose(0, 2, 1).reshape(1, 2 * FR)  1.86 us

profile of v3, /device:TPU:0, one launch (start us, length us, event | category | flops | bytes accessed | tf_op | source)
XLA Modules:
  0.0 59.9 jit_solution(8276468283595805494)
XLA Ops:
  0.0 58.1 %shard_map.100 = f32[16,512]{1,0:T(8,128)} custom-call(bf16[8,16,4096]{2,1,0:T(8,128)(2,1)} %bitcast.7, bf16[8,16,512]{2,1,0:T(8,128)(2,1)} %bitcast.9, s32[1,4]{1,0:T(1,128)} %bitcast.10, s32[1,32]{1,0:T(1,128)} %bitcast.11, bf16[1024,1024]{1,0:T(8,128)(2,1)} %constant.12.clone.refs_0_, bf16[512,1024]{1,0:T(8,128)(2,1)} %constant.13.clone.refs_1_, ...), custom_call_target="tpu_custom_call" | custom-call | tf_op jit(solution)/shard_map/pallas_call | solution.py:509
  58.1 1.0 %copy.12 = f32[2,8,512]{1,2,0:T(8,128)S(1)} copy(f32[2,8,512]{2,1,0:T(8,128)} %bitcast.8) | data formatting | bytes 65536 | tf_op jit(solution)/shard_map/reshape | solution.py:547
  59.0 0.9 %reshape.19 = f32[1,8192]{1,0:T(1,128)} reshape(f32[2,512,8]{2,1,0:T(8,128)S(1)} %bitcast.6) | data formatting | bytes 65536 | tf_op jit(solution)/shard_map/reshape | solution.py:547

commit v4 on v3

--- a/solution.py
+++ b/solution.py
@@ -310,29 +310,12 @@
             sent(taps.at[to, :, share], tin.at[me, :, share], t_send.at[o], t_recv.at[o], chan=to)
         )
         tap_copies[-1].start()
-        x_copy(o).start()
     for o in far_first:
         id_copies.append(sent(ids, ids_in.at[o], ids_send.at[o], ids_recv.at[o], chan=partner(o)))
         id_copies[-1].start()
-    for copy in own + loads:
-        copy.wait()
-
-    def take(block):
-        rows = pl.ds(pl.multiple_of(block * per, per), per)
-        flat = jnp.concatenate([xin[block, :, q * span : (q + 1) * span] for q in range(FR // span)], axis=0)
-        got = jnp.dot(flat, pick[...], preferred_element_type=jnp.float32).astype(jnp.bfloat16)
-        for q in range(FR // span):
-            for n in range(SPLIT):
-                xd[n * per : (n + 1) * per, q * LANES : (q + 1) * LANES] = got[
-                    q * per : (q + 1) * per, n * LANES : (n + 1) * LANES
-                ]
-        found = jnp.dot(xd[...], high[...], preferred_element_type=jnp.float32) + jnp.dot(
-            xd[...], low[...], preferred_element_type=jnp.float32
-        )
-        for n in range(SPLIT):
-            fx[n, rows, :] = found[n * per : (n + 1) * per]
-
-    take(me)
+    for o in range(1, chan):
+        x_copy(o).start()
+    own[1].wait()
     for copy in tap_copies:
         copy.wait_recv()
     forwards = []
@@ -340,59 +323,22 @@
         to = lax.rem(my_hour + o, hour)
         forwards.append(sent(tin.at[:, :, share], tin.at[:, :, share], f_send.at[o], f_recv.at[o], hour=to))
         forwards[-1].start()
-
-    @pl.loop(1, chan // 2)
-    def _(o):
-        x_copy(o).wait_recv()
-        take(partner(o))
-
-    for copy in forwards:
-        copy.wait_recv()
-    count = tin.shape[2]
-    got = jnp.dot(
-        tin[...].reshape(chan * per, count), pick[:count, :], preferred_element_type=jnp.float32
-    ).astype(jnp.bfloat16)
-    for n in range(SPLIT):
-        td[n] = got[:, n * LANES : (n + 1) * LANES]
-
-    @pl.loop(0, SPLIT)
-    def _(n):
-        fh[n] = jnp.dot(td[n], high[:LANES, :], preferred_element_type=jnp.float32) + jnp.dot(
-            td[n], low[:LANES, :], preferred_element_type=jnp.float32
-        )
-
-    for copy in id_copies:
-        copy.wait_recv()
-    labels = ids[...]
-    for o in range(1, chan):
-        labels = labels + ids_in[o]
-    onehot = rows_of_pairs(labels, owners, chan, hour)
-    cross[...] = jnp.zeros_like(cross)
-
-    @pl.loop(chan // 2, chan)
-    def _(o):
-        x_copy(o).wait_recv()
-        take(partner(o))
-
-    pairs = pairs_of(chan)
+    for copy in loads + own[:1]:
+        copy.wait()
+
     lane0 = lax.broadcasted_iota(jnp.int32, (8, LANES), 1) == 0
-    steps = SPLIT // 2
-
-    def part_copy(t, o):
-        to = lax.rem(my_hour + o, hour)
-        where = pl.ds(t * steps, steps)
-        return sent(part.at[to, where], first.at[o, where], send.at[t, o], recv.at[t, o], hour=to)
-
-    def tile(t, edge):
-        @pl.loop(0, chan * per // 8)
+
+    def spectra(block, t, edge):
+        @pl.loop(0, per // 8)
         def _(g):
-            here = pl.ds(pl.multiple_of(8 * g, 8), 8)
-
-            def bins_of(f):
+            piece = pl.ds(pl.multiple_of(8 * g, 8), 8)
+            here = pl.ds(pl.multiple_of(block * per + 8 * g, 8), 8)
+
+            def bins_of(f, rows):
                 values, extra = [], []
                 for n in range(SPLIT):
-                    re = f[n, here, pl.ds(pl.multiple_of(2 * t * LANES, LANES), LANES)]
-                    im = f[n, here, pl.ds(pl.multiple_of((2 * t + 1) * LANES, LANES), LANES)]
+                    re = f[n, rows, pl.ds(pl.multiple_of(2 * t * LANES, LANES), LANES)]
+                    im = f[n, rows, pl.ds(pl.multiple_of((2 * t + 1) * LANES, LANES), LANES)]
                     if edge:
                         angle = -math.pi * n / SPLIT
                         extra.append((im * math.cos(angle), im * math.sin(angle)))
@@ -412,13 +358,77 @@
                         )
                 return found
 
-            freq = bins_of(fx)
-            resp = bins_of(fh)
+            freq = bins_of(fx, piece)
+            resp = bins_of(fh, here)
             for k2 in range(SPLIT):
                 (xr, xi), (hr, hi) = freq[k2], resp[k2]
-                spec[k2, 0, here, :] = (xr * hr - xi * hi).astype(jnp.bfloat16).astype(jnp.float32)
-                spec[k2, 1, here, :] = (xr * hi + xi * hr).astype(jnp.bfloat16).astype(jnp.float32)
-
+                spec[t, k2, 0, here, :] = (xr * hr - xi * hi).astype(jnp.bfloat16).astype(jnp.float32)
+                spec[t, k2, 1, here, :] = (xr * hi + xi * hr).astype(jnp.bfloat16).astype(jnp.float32)
+
+    def take(block):
+        flat = jnp.concatenate([xin[block, :, q * span : (q + 1) * span] for q in range(FR // span)], axis=0)
+        got = jnp.dot(flat, pick[...], preferred_element_type=jnp.float32).astype(jnp.bfloat16)
+        for q in range(FR // span):
+            for n in range(SPLIT):
+                xd[n * per : (n + 1) * per, q * LANES : (q + 1) * LANES] = got[
+                    q * per : (q + 1) * per, n * LANES : (n + 1) * LANES
+                ]
+        found = jnp.dot(xd[...], high[...], preferred_element_type=jnp.float32) + jnp.dot(
+            xd[...], low[...], preferred_element_type=jnp.float32
+        )
+        for n in range(SPLIT):
+            fx[n] = found[n * per : (n + 1) * per]
+        spectra(block, 0, True)
+
+        @pl.loop(1, TILES)
+        def _(t):
+            spectra(block, t, False)
+
+    for copy in forwards:
+        copy.wait_recv()
+    count = tin.shape[2]
+    got = jnp.dot(
+        tin[...].reshape(chan * per, count), pick[:count, :], preferred_element_type=jnp.float32
+    ).astype(jnp.bfloat16)
+    for n in range(SPLIT):
+        td[n] = got[:, n * LANES : (n + 1) * LANES]
+
+    @pl.loop(0, SPLIT)
+    def _(n):
+        fh[n] = jnp.dot(td[n], high[:LANES, :], preferred_element_type=jnp.float32) + jnp.dot(
+            td[n], low[:LANES, :], preferred_element_type=jnp.float32
+        )
+
+    for copy in id_copies:
+        copy.wait_recv()
+    labels = ids[...]
+    for o in range(1, chan):
+        labels = labels + ids_in[o]
+    onehot = rows_of_pairs(labels, owners, chan, hour)
+    cross[...] = jnp.zeros_like(cross)
+
+    take(me)
+
+    @pl.loop(1, chan // 2)
+    def _(o):
+        x_copy(o).wait_recv()
+        take(partner(o))
+
+    @pl.loop(chan // 2, chan)
+    def _(o):
+        x_copy(o).wait_recv()
+        take(partner(o))
+
+    pairs = pairs_of(chan)
+    steps = SPLIT // 2
+
+    def part_copy(t, o):
+        to = lax.rem(my_hour + o, hour)
+        where = pl.ds(t * steps, steps)
+        return sent(part.at[to, where], first.at[o, where], send.at[t, o], recv.at[t, o], hour=to)
+
+    @pl.loop(0, TILES)
+    def _(t):
         @pl.loop(0, steps)
         def _(kk):
             both = []
@@ -430,8 +440,8 @@
                     for c in range(per // 8):
                         near = pl.ds(i * per + 8 * c, 8)
                         far = pl.ds((i - r - 1) * per + 8 * c, 8)
-                        nr, ni = spec[k2, 0, near, :], spec[k2, 1, near, :]
-                        fr, fi = spec[k2, 0, far, :], spec[k2, 1, far, :]
+                        nr, ni = spec[t, k2, 0, near, :], spec[t, k2, 1, near, :]
+                        fr, fi = spec[t, k2, 0, far, :], spec[t, k2, 1, far, :]
                         one, two = fr * nr + fi * ni, fi * nr - fr * ni
                         re, im = (one, two) if re is None else (re + one, im + two)
                     cross[8 * p : 8 * p + 8, :LANES] = re
@@ -451,12 +461,6 @@
 
         for o in range(1, hour):
             part_copy(t, o).start()
-
-    tile(0, True)
-
-    @pl.loop(1, TILES)
-    def _(t):
-        tile(t, False)
 
     width = 2 * LANES
     depth = chan * TILES * SPLIT
@@ -519,9 +523,9 @@
             pltpu.VMEM((chan, 8, depth), jnp.int32),
             pltpu.VMEM((SPLIT * per, SUB), jnp.bfloat16),
             pltpu.VMEM((SPLIT, channels, LANES), jnp.bfloat16),
+            pltpu.VMEM((SPLIT, per, 2 * SUB), jnp.float32),
             pltpu.VMEM((SPLIT, channels, 2 * SUB), jnp.float32),
-            pltpu.VMEM((SPLIT, channels, 2 * SUB), jnp.float32),
-            pltpu.VMEM((SPLIT, 2, channels, LANES), jnp.float32),
+            pltpu.VMEM((TILES, SPLIT, 2, channels, LANES), jnp.float32),
             pltpu.VMEM((depth, 2 * LANES), jnp.float32),
             pltpu.VMEM(part, jnp.bfloat16),
             pltpu.VMEM(part, jnp.bfloat16),

time: 60.1 us -> 51.8 us (0.86)
  Pallas kernels: 58.1 us -> 49.7 us
    pallas_call x1, Pallas kernels: 58.1 us -> 49.7 us  [split_body(): pl.pallas_call(functools.partial(kernel, chan, hour, norm), out_shape=jax...]
where the time goes in v4:
time: 51.8 us; the launch traced here: 51.6 us
  Pallas kernels  49.7 us (96%)
  local copies, waits for them, and re-layouts  1.86 us (4%)
    pallas_call x1, Pallas kernels, split_body(): pl.pallas_call(functools.partial(kernel, chan, hour, norm), out_shape=jax...  49.7 us
    reshape x2, local copies, waits for them, and re-layouts, split_body(): return wave.reshape(2, SPLIT, SUB).transpose(0, 2, 1).reshape(1, 2 * FR)  1.86 us

profile of v4, /device:TPU:0, one launch (start us, length us, event | category | flops | bytes accessed | tf_op | source)
XLA Modules:
  0.0 51.6 jit_solution(8806901127407343985)
XLA Ops:
  0.0 49.7 %shard_map.100 = f32[16,512]{1,0:T(8,128)} custom-call(bf16[8,16,4096]{2,1,0:T(8,128)(2,1)} %bitcast.7, bf16[8,16,512]{2,1,0:T(8,128)(2,1)} %bitcast.9, s32[1,4]{1,0:T(1,128)} %bitcast.10, s32[1,32]{1,0:T(1,128)} %bitcast.11, bf16[1024,1024]{1,0:T(8,128)(2,1)} %constant.12.clone.refs_0_, bf16[512,1024]{1,0:T(8,128)(2,1)} %constant.13.clone.refs_1_, ...), custom_call_target="tpu_custom_call" | custom-call | tf_op jit(solution)/shard_map/pallas_call | solution.py:513
  49.8 1.0 %copy.12 = f32[2,8,512]{1,2,0:T(8,128)S(1)} copy(f32[2,8,512]{2,1,0:T(8,128)} %bitcast.8) | data formatting | bytes 65536 | tf_op jit(solution)/shard_map/reshape | solution.py:551
  50.7 0.9 %reshape.19 = f32[1,8192]{1,0:T(1,128)} reshape(f32[2,512,8]{2,1,0:T(8,128)S(1)} %bitcast.6) | data formatting | bytes 65536 | tf_op jit(solution)/shard_map/reshape | solution.py:551
